TPU v7x, 256 devices: a whole 4x4x8 slice. The times are simulated.
256 devices in a mesh: fsdp: 16 (over x_lo, y, core), seq: 16 (over x_hi, z).
Axes of the slice: x: 4 (x_hi: 2, x_lo: 2; x = x_hi * 2 + x_lo), y: 4, z: 8, core: 2. Of those that a mesh axis runs over, the one named last changes fastest.
Arguments:
- attn_inputs: bfloat16 [16, 2048, 3, 2048], P('fsdp', 'seq'), may hold values from -32 to 32
- out_weight: bfloat16 [2048, 3072], P('fsdp'), may hold values from -0.125 to 0.125
- skew_params: float32 [96, 128, 128], P('fsdp'), may hold values from -0.3 to 0.3
- piece_orders: int32 [4, 96], replicated, may hold values from 0 to 95, each once within a row
- cotangent: bfloat16 [16, 2048, 3072], P('fsdp', 'seq'), may hold values from -6 to 6
Outputs:
- block_output: bfloat16 [16, 2048, 3072], P('fsdp', 'seq')
- grad_inputs: bfloat16 [16, 2048, 3, 2048], P('fsdp', 'seq')
- grad_skew: float32 [96, 128, 128], P('fsdp')
Inputs may be any that keep to these rules, and one draw needn't show every extreme that they name: `piece_orders`: each row lists every piece number from 0 to 95 exactly once.
All inputs are finite; a program needn't handle non-finite values.
Results may differ from a plain program's by a relative error of at most 0.03.
Values may be sent and summed in bfloat16 or wider, within the bound.
No kernel may reach another device: no remote copies, remote signals or barrier semaphores. Data moves between devices by JAX's collectives and lax.ppermute only.
A program may use at most 128 MiB of HBM per device.

v0:
```python
import math

import jax
import jax.numpy as jnp
from jax import lax
from jax.sharding import PartitionSpec as P

HEADS = 16
HD = 128
BS = 128
FACTORS = 4


def cayley(skew_params):
    skewed = skew_params - jnp.swapaxes(skew_params, -1, -2)
    identity = jnp.eye(skew_params.shape[-1], dtype=skew_params.dtype)
    minus_part = identity - skewed
    gram_matrix = identity + jnp.matmul(
        jnp.swapaxes(skewed, -1, -2), skewed, precision=lax.Precision.HIGHEST
    )
    factor_low = jnp.linalg.cholesky(gram_matrix)
    halfway = lax.linalg.triangular_solve(factor_low, minus_part, left_side=True, lower=True)
    solved = lax.linalg.triangular_solve(
        factor_low, halfway, left_side=True, lower=True, transpose_a=True
    )
    return jnp.matmul(minus_part, solved, precision=lax.Precision.HIGHEST)


def reorder(matrix, ordering):
    row_count = matrix.shape[0]
    return jnp.take(matrix.reshape(row_count, ordering.shape[0], -1), ordering, axis=1).reshape(
        row_count, -1
    )


def inverse_order(ordering):
    return jnp.zeros_like(ordering).at[ordering].set(jnp.arange(ordering.shape[0], dtype=jnp.int32))


def local(attn_inputs, out_weight, skew_params, piece_orders, cotangent):
    seq_count = lax.axis_size("seq")
    tok_count = attn_inputs.shape[1]
    full_width = attn_inputs.shape[3]
    model_width = out_weight.shape[1]
    heads_here = HEADS // seq_count
    group_width = heads_here * HD
    length_all = tok_count * seq_count
    scaling = 1.0 / math.sqrt(HD)
    blocks_per = model_width // BS
    weight_full = lax.all_gather(out_weight, "fsdp", axis=0, tiled=True)
    rot_own = cayley(skew_params).astype(jnp.bfloat16)
    rotations = lax.all_gather(rot_own, "fsdp", axis=0, tiled=True).reshape(
        FACTORS, blocks_per, BS, BS
    )
    local_rows = attn_inputs[0].reshape(tok_count, 3, seq_count, group_width)
    spread = lax.all_to_all(local_rows, "seq", split_axis=2, concat_axis=0, tiled=True)
    queries = spread[:, 0]
    key_rows = spread[:, 1]
    value_rows = spread[:, 2]
    block_rows = min(512, length_all)
    block_count = length_all // block_rows
    query_blocks = queries.reshape(block_count, block_rows, heads_here, HD)

    def forward_block(query_block):
        scores = (
            jnp.einsum("qhd,khd->hqk", query_block, key_rows, preferred_element_type=jnp.float32)
            * scaling
        )
        shifted = jnp.exp(scores - jnp.max(scores, axis=-1, keepdims=True))
        rounded = (shifted / jnp.sum(shifted, axis=-1, keepdims=True)).astype(jnp.bfloat16)
        wide_out = jnp.einsum(
            "hqk,khd->qhd", rounded, value_rows, preferred_element_type=jnp.float32
        )
        return (wide_out.astype(jnp.bfloat16), wide_out, rounded)

    attended, wide_blocks, rounded_blocks = lax.map(forward_block, query_blocks)
    attended = attended.reshape(length_all, 1, group_width)
    attended = lax.all_to_all(attended, "seq", split_axis=0, concat_axis=1, tiled=True).reshape(
        tok_count, full_width
    )
    projected = jnp.dot(attended, weight_full, preferred_element_type=jnp.float32).astype(
        jnp.bfloat16
    )
    current = projected
    saved_rows = []
    for factor in range(FACTORS):
        ordering = piece_orders[factor]
        moved_rows = reorder(current, ordering).reshape(tok_count, blocks_per, BS)
        saved_rows.append(moved_rows)
        mixed_rows = jnp.einsum(
            "tjb,jbc->tjc", moved_rows, rotations[factor], preferred_element_type=jnp.float32
        )
        current = reorder(
            mixed_rows.reshape(tok_count, model_width), inverse_order(ordering)
        ).astype(jnp.bfloat16)
    block_output = current.reshape(1, tok_count, model_width)
    upstream = cotangent[0]
    pieces_grad = [None] * FACTORS
    for factor in reversed(range(FACTORS)):
        ordering = piece_orders[factor]
        moved_grad = reorder(upstream, ordering).reshape(tok_count, blocks_per, BS)
        pieces_grad[factor] = jnp.einsum(
            "tjb,tjc->jbc", saved_rows[factor], moved_grad, preferred_element_type=jnp.float32
        )
        back_mixed = jnp.einsum(
            "tjc,jbc->tjb", moved_grad, rotations[factor], preferred_element_type=jnp.float32
        )
        upstream = reorder(
            back_mixed.reshape(tok_count, model_width), inverse_order(ordering)
        ).astype(jnp.bfloat16)
    rot_grad = jnp.stack(pieces_grad).reshape(FACTORS * blocks_per, BS, BS)
    grad_attended = lax.dot_general(
        upstream, weight_full, (((1,), (1,)), ((), ())), preferred_element_type=jnp.float32
    ).astype(jnp.bfloat16)
    grad_spread = lax.all_to_all(
        grad_attended.reshape(tok_count, seq_count, group_width),
        "seq",
        split_axis=1,
        concat_axis=0,
        tiled=True,
    )
    grad_spread = grad_spread.reshape(block_count, block_rows, heads_here, HD)

    def backward_block(carry, items):
        key_acc, value_acc = carry
        query_block, dout_block, rounded, wide_out = items
        dprobs = jnp.einsum(
            "qhd,khd->hqk", dout_block, value_rows, preferred_element_type=jnp.float32
        )
        centre = jnp.einsum("qhd,qhd->hq", dout_block.astype(jnp.float32), wide_out)[:, :, None]
        dscores = (rounded.astype(jnp.float32) * (dprobs - centre) * scaling).astype(jnp.bfloat16)
        grad_q = jnp.einsum(
            "hqk,khd->qhd", dscores, key_rows, preferred_element_type=jnp.float32
        ).astype(jnp.bfloat16)
        key_acc = key_acc + jnp.einsum(
            "hqk,qhd->khd", dscores, query_block, preferred_element_type=jnp.float32
        )
        value_acc = value_acc + jnp.einsum(
            "hqk,qhd->khd", rounded, dout_block, preferred_element_type=jnp.float32
        )
        return ((key_acc, value_acc), grad_q)

    zero_acc = jnp.zeros((length_all, heads_here, HD), jnp.float32)
    (key_acc, value_acc), query_grads = lax.scan(
        backward_block,
        (zero_acc, zero_acc),
        (query_blocks, grad_spread, rounded_blocks, wide_blocks),
    )
    stacked = jnp.stack(
        [
            query_grads.reshape(length_all, group_width),
            key_acc.astype(jnp.bfloat16).reshape(length_all, group_width),
            value_acc.astype(jnp.bfloat16).reshape(length_all, group_width),
        ],
        axis=1,
    )
    stacked = stacked.reshape(length_all, 3, 1, group_width)
    grad_inputs = lax.all_to_all(stacked, "seq", split_axis=0, concat_axis=2, tiled=True).reshape(
        1, tok_count, 3, full_width
    )
    block_share = lax.psum_scatter(
        rot_grad.astype(jnp.bfloat16), "fsdp", scatter_dimension=0, tiled=True
    )
    owner_grad = lax.psum(block_share, "seq").astype(jnp.float32)
    total_tokens = lax.axis_size("fsdp") * length_all
    unused, pullback = jax.vjp(cayley, skew_params)
    grad_skew = pullback(owner_grad * (1.0 / math.sqrt(total_tokens)))[0]
    return (block_output, grad_inputs, grad_skew)


def solution(mesh):
    in_specs = (
        P("fsdp", "seq", None, None),
        P("fsdp", None),
        P("fsdp", None, None),
        P(),
        P("fsdp", "seq", None),
    )
    out_specs = (P("fsdp", "seq", None), P("fsdp", "seq", None, None), P("fsdp", None, None))
    return jax.shard_map(local, mesh=mesh, in_specs=in_specs, out_specs=out_specs, check_vma=False)
```

profile of v0, /device:TPU:24, one launch (start us, length us, event | category | flops | bytes accessed | tf_op | source)
XLA Modules:
  0.0 698.0 jit_solution(13345446725951341136)
XLA Ops:
  10.6 70.3 %custom-call.23 = f32[6,128,128]{2,1,0:T(8,128)S(1)} custom-call(f32[6,128,128]{2,1,0:T(8,128)S(1)} %fusion.64), custom_call_target="Cholesky" | custom-call | tf_op jit(solution)/shard_map/jit(cholesky)/cholesky/custom-call.1 | solution.py:21
  82.6 58.9 %custom-call.25 = f32[6,1,128,128]{2,3,1,0:T(8,128)S(1)} custom-call(f32[6,1,128,128]{3,2,1,0:T(8,128)S(1)} %get-tuple-element.302), custom_call_target="InvertDiagBlocksLowerTriangular" | custom-call | tf_op jit(solution)/shard_map/triangular_solve/custom-call.0 | solution.py:23
  147.5 11.0 %all-to-all-start = ((bf16[128,3,16,128]{3,0,1,2:T(8,128)(2,1)}), bf16[128,3,16,128]{3,0,1,2:T(8,128)(2,1)S(1)}, u32[]{:S(2)}, u32[]{:S(2)}) async-start(bf16[128,3,16,128]{3,0,1,2:T(8,128)(2,1)} %copy.274), calls=%async_computation | async-start | bytes 3145728 | tf_op jit(solution)/shard_map/all_to_all | solution.py:56
  162.5 35.6 %all-to-all-done = bf16[128,3,16,128]{3,0,1,2:T(8,128)(2,1)S(1)} async-done(((bf16[128,3,16,128]{3,0,1,2:T(8,128)(2,1)}), bf16[128,3,16,128]{3,0,1,2:T(8,128)(2,1)S(1)}, u32[]{:S(2)}, u32[]{:S(2)}) %all-to-all-start) | async-done | bytes 1572896 | tf_op jit(solution)/shard_map/all_to_all | solution.py:56
  198.5 21.2 %while.29 = (s32[]{:T(128)}, bf16[4,512,1,128]{3,1,2,0:T(8,128)(2,1)S(1)}, f32[4,512,1,128]{3,1,2,0:T(8,128)}, bf16[4,1,512,2048]{3,2,1,0:T(8,128)(2,1)}, bf16[4...) while((s32[]{:T(128)}, ...), condition=%wide.region_5.9_spmd, body=%wide.region_2.8_spmd.sunk | while | flops 546372608 | bytes 20982876 | solution.py:76
  222.5 4.9 all-to-all-start.1
  228.7 15.6 %all-to-all-done.1 = bf16[16,2,8192]{2,1,0:T(2,128)(2,1)S(1)} async-done(((bf16[16,2,8192]{2,1,0:T(2,128)(2,1)}), bf16[16,2,8192]{2,1,0:T(2,128)(2,1)S(1)}, u32[]{:S(2)}, u32[]{:S(2)}) %all-to-all-start.1) | async-done | bytes 524320 | tf_op jit(solution)/shard_map/all_to_all | solution.py:78
  249.3 2.9 gather_fusion.10
  254.8 2.7 gather_fusion.11
  259.7 2.8 gather_fusion.12
  265.1 2.7 gather_fusion.13
  270.1 2.7 gather_fusion.14
  272.8 7.1 %all-gather.5.cloned.1.call-done = bf16[2048,3072]{1,0:T(8,128)(2,1)} async-done(((bf16[128,3072]{1,0:T(8,128)(2,1)}), bf16[2048,3072]{1,0:T(8,128)(2,1)}) %all-gather.5.cloned.1.call-update) | async-done | bytes 12582928 | tf_op jit(solution)/shard_map/all_gather | solution.py:50
  279.9 7.5 %convolution_convert_fusion.1 = bf16[128,3072]{1,0:T(8,128)(2,1)} fusion(bf16[128,2048]{0,1:T(8,128)(2,1)} %bitcast.438, bf16[2048,3072]{1,0:T(8,128)(2,1)} %all-gather.5.cloned.1.call-done), kind=kOutput, calls=%fused_computation.60 | convolution fusion | flops 1611005952 | bytes 13893632 | tf_op jit(solution)/shard_map/dot_general | solution.py:81
  289.7 2.7 gather_fusion
  296.9 2.7 gather_fusion.1
  299.6 2.4 fusion.112
  302.0 2.7 gather_fusion.15
  304.7 2.9 bitcast_convert_fusion.1
  307.6 2.7 gather_fusion.2
  313.0 2.7 gather_fusion.3
  317.9 2.7 gather_fusion.4
  323.3 2.7 gather_fusion.5
  328.3 17.7 %fusion.32 = bf16[16,16,8,128]{3,2,1,0:T(8,128)(2,1)S(1)} fusion(bf16[128,3072]{0,1:T(8,128)(2,1)} %bitcast.437, bf16[2048,3072]{1,0:T(8,128)(2,1)} %all-gather.5.cloned.1.call-done), kind=kOutput, calls=%fused_computation.80 | convolution fusion | flops 1610874880 | bytes 13893632 | tf_op jit(solution)/shard_map/dot_general | solution.py:112
  347.0 9.3 %all-to-all-start.2 = ((bf16[128,16,128]{2,0,1:T(8,128)(2,1)}), bf16[128,16,128]{2,0,1:T(8,128)(2,1)}, u32[]{:S(2)}, u32[]{:S(2)}) async-start(bf16[128,16,128]{2,0,1:T(8,128)(2,1)} %bitcast.440), calls=%async_computation.2 | async-start | bytes 1048576 | tf_op jit(solution)/shard_map/all_to_all | solution.py:115
  356.4 2.9 fusion.29
  359.3 2.7 gather_fusion.6
  368.9 4.7 copy.307
  374.6 57.2 %while.30 = (s32[]{:T(128)}, f32[2048,1,128]{0,2,1:T(8,128)}, f32[2048,1,128]{0,2,1:T(8,128)}, bf16[4,512,1,128]{3,1,2,0:T(8,128)(2,1)}, bf16[4,512,1,128]{3,1,2...) while((s32[]{:T(128)}, f32[2048,1,128]{0,2,1:T(8,128)}, ...), condition=%wide.region_11.17_spmd.clone, body=%wide.region_10.16_spmd.clone.sunk | while | flops 1080294912 | bytes 27663552 | solution.py:144
  376.6 3.9 multiply_convert_fusion.2
  380.6 3.3 fusion.189
  385.2 3.4 fusion.190
  390.6 4.0 multiply_convert_fusion.2
  394.6 3.5 fusion.189
  399.5 3.5 fusion.190
  405.0 4.0 multiply_convert_fusion.2
  409.0 3.5 fusion.189
  413.9 3.5 fusion.190
  419.4 3.9 multiply_convert_fusion.2
  423.4 3.5 fusion.189
  428.3 3.5 fusion.190
  437.9 10.7 %copy.299 = bf16[2048,3,1,128]{3,1,2,0:T(4,128)(2,1)} copy(bf16[2048,3,1,128]{3,0,1,2:T(8,128)(2,1)S(1)} %maximum_bitcast_fusion) | data formatting | bytes 3145728 | tf_op jit(solution)/shard_map/reshape | solution.py:157
  448.6 9.5 %all-to-all-start.3 = ((bf16[2048,3,1,128]{3,1,2,0:T(4,128)(2,1)}), bf16[2048,3,1,128]{3,1,2,0:T(4,128)(2,1)}, u32[]{:S(2)}, u32[]{:S(2)}) async-start(bf16[2048,3,1,128]{3,1,2,0:T(4,128)(2,1)} %copy.299), calls=%async_computation.3 | async-start | bytes 4194304 | tf_op jit(solution)/shard_map/all_to_all | solution.py:158
  458.2 60.6 %custom-call.28 = f32[6,1,128,128]{2,3,1,0:T(8,128)} custom-call(f32[6,1,128,128]{3,2,1,0:T(8,128)} %get-tuple-element.301), custom_call_target="InvertDiagBlocksLowerTriangular" | custom-call | tf_op jit(solution)/shard_map/transpose(jvp())/triangular_solve/custom-call.3 | solution.py:23
  522.6 2.3 fusion.52
  524.9 2.4 fusion.108
  530.7 2.9 copy.300
  536.0 143.0 %all-reduce.2.cloned.1.call-done = bf16[6,128,128]{1,2,0:T(8,128)(2,1)} async-done(((bf16[6,128,128]{1,2,0:T(8,128)(2,1)}), bf16[6,128,128]{1,2,0:T(8,128)(2,1)}) %all-reduce.2.cloned.1.call-update) | async-done | bytes 196624 | tf_op jit(solution)/shard_map/psum | solution.py:164
  (242 shorter events, 121.2 us)
Async XLA Ops:
  7.2 238.8 %all-gather.3.cloned.1.call-start = ((), (), s32[]{:S(2)}) async-start(), calls=%async_computation.5 | async-start | bytes 3342336 | tf_op jit(solution)/shard_map/all_gather | solution.py:52
  7.2 135.7 %copy-start.24 = (f32[128,128]{1,0:T(8,128)}, f32[128,128]{1,0:T(8,128)S(1)}, u32[]{:S(2)}) copy-start(f32[128,128]{1,0:T(8,128)S(1)} %get-tuple-element.320) | copy-start | bytes 196612
  9.5 133.5 %copy-start.3 = (f32[6,128,128]{2,1,0:T(8,128)}, f32[6,128,128]{2,1,0:T(8,128)S(1)}, u32[]{:S(2)}) copy-start(f32[6,128,128]{2,1,0:T(8,128)S(1)} %bitcast_subtract_fusion) | copy-start | bytes 1179652
  10.5 134.4 %copy-start.25 = (bf16[1,128,3,2048]{3,1,2,0:T(8,128)(2,1)S(1)}, bf16[1,128,3,2048]{3,1,2,0:T(8,128)(2,1)}, u32[]{:S(2)}) copy-start(bf16[1,128,3,2048]{3,1,2,0:T(8,128)(2,1)} %param.18) | copy-start | bytes 4718596
  80.9 1.8 copy-start.26
  81.1 63.2 %copy-start.37 = (pred[6]{0:T(512)(128)(4,1)}, pred[6]{0:T(512)(128)(4,1)S(1)}, u32[]{:S(2)}) copy-start(pred[6]{0:T(512)(128)(4,1)S(1)} %compare_reduce_fusion) | copy-start | bytes 22
  141.6 2.7 copy-start.17
  144.2 135.7 %all-gather.5.cloned.1.call-start = ((), (), s32[]{:S(2)}) async-start(), calls=%async_computation.6 | async-start | bytes 13369344 | tf_op jit(solution)/shard_map/all_gather | solution.py:50
  145.9 12.6 %copy-start.36 = (s32[4,96]{1,0:T(4,128)S(1)}, s32[4,96]{1,0:T(4,128)}, u32[]{:S(2)}) copy-start(s32[4,96]{1,0:T(4,128)} %param.21) | copy-start | bytes 4612
  147.5 50.6 %all-to-all-start = ((bf16[128,3,16,128]{3,0,1,2:T(8,128)(2,1)}), bf16[128,3,16,128]{3,0,1,2:T(8,128)(2,1)S(1)}, u32[]{:S(2)}, u32[]{:S(2)}) async-start(bf16[128,3,16,128]{3,0,1,2:T(8,128)(2,1)} %copy.274), calls=%async_computation | async-start | bytes 3145728 | tf_op jit(solution)/shard_map/all_to_all | solution.py:56
  219.7 7.7 %copy-start.16 = (bf16[4,512,1,128]{3,1,2,0:T(8,128)(2,1)}, bf16[4,512,1,128]{3,1,2,0:T(8,128)(2,1)S(1)}, u32[]{:S(2)}) copy-start(bf16[4,512,1,128]{3,1,2,0:T(8,128)(2,1)S(1)} %get-tuple-element.514) | copy-start | bytes 1572868
  219.7 8.1 %copy-start.5 = (bf16[2048,1,128]{2,0,1:T(8,128)(2,1)}, bf16[2048,1,128]{2,0,1:T(8,128)(2,1)S(1)}, u32[]{:S(2)}) copy-start(bf16[2048,1,128]{2,0,1:T(8,128)(2,1)S(1)} %get-tuple-element.509) | copy-start | bytes 1572868
  219.7 8.8 %copy-start.2 = (bf16[2048,1,128]{2,0,1:T(8,128)(2,1)}, bf16[2048,1,128]{2,0,1:T(8,128)(2,1)S(1)}, u32[]{:S(2)}) copy-start(bf16[2048,1,128]{2,0,1:T(8,128)(2,1)S(1)} %get-tuple-element.508) | copy-start | bytes 1572868
  219.7 7.7 %copy-start.28 = (bf16[1,128,3072]{2,1,0:T(8,128)(2,1)S(1)}, bf16[1,128,3072]{2,1,0:T(8,128)(2,1)}, u32[]{:S(2)}) copy-start(bf16[1,128,3072]{2,1,0:T(8,128)(2,1)} %param.22) | copy-start | bytes 2359300
  222.5 21.8 %all-to-all-start.1 = ((bf16[16,2,8192]{2,1,0:T(2,128)(2,1)}), bf16[16,2,8192]{2,1,0:T(2,128)(2,1)S(1)}, u32[]{:S(2)}, u32[]{:S(2)}) async-start(bf16[16,2,8192]{2,1,0:T(2,128)(2,1)} %reshape.569), calls=%async_computation.1 | async-start | bytes 1048576 | tf_op jit(solution)/shard_map/all_to_all | solution.py:78
  228.7 18.7 %copy-start.8 = (bf16[96,128,32]{1,2,0:T(8,128)(2,1)}, bf16[96,128,32]{1,2,0:T(8,128)(2,1)S(1)}, u32[]{:S(2)}) copy-start(bf16[96,128,32]{1,2,0:T(8,128)(2,1)S(1)} %broadcast_select_fusion) | copy-start | bytes 2359300
  249.3 4.2 copy-start
  294.0 2.9 copy-start.15
  311.6 1.4 copy-start.13
  322.0 1.3 copy-start.14
  347.0 26.7 %all-to-all-start.2 = ((bf16[128,16,128]{2,0,1:T(8,128)(2,1)}), bf16[128,16,128]{2,0,1:T(8,128)(2,1)}, u32[]{:S(2)}, u32[]{:S(2)}) async-start(bf16[128,16,128]{2,0,1:T(8,128)(2,1)} %bitcast.440), calls=%async_computation.2 | async-start | bytes 1048576 | tf_op jit(solution)/shard_map/all_to_all | solution.py:115
  356.3 173.0 %reduce-scatter.2.cloned.1.call-start = ((), (), s32[]{:S(2)}) async-start(), calls=%async_computation.7 | async-start | bytes 3342336 | tf_op jit(solution)/shard_map/reduce_scatter | solution.py:161
  362.0 4.4 copy-start.9
  362.0 5.1 copy-start.22
  362.0 5.1 copy-start.23
  380.6 3.3 copy-start.1
  380.6 3.3 copy-start.6
  394.6 3.6 copy-start.1
  394.6 3.6 copy-start.6
  409.0 3.6 copy-start.1
  409.0 3.6 copy-start.6
  423.4 3.6 copy-start.1
  423.4 3.6 copy-start.6
  437.9 82.2 %copy-start.4 = (f32[6,128,128]{2,1,0:T(8,128)S(1)}, f32[6,128,128]{2,1,0:T(8,128)}, u32[]{:S(2)}) copy-start(f32[6,128,128]{2,1,0:T(8,128)} %copy-done.3) | copy-start | bytes 1179652
  448.6 82.1 %all-to-all-start.3 = ((bf16[2048,3,1,128]{3,1,2,0:T(4,128)(2,1)}), bf16[2048,3,1,128]{3,1,2,0:T(4,128)(2,1)}, u32[]{:S(2)}, u32[]{:S(2)}) async-start(bf16[2048,3,1,128]{3,1,2,0:T(4,128)(2,1)} %copy.299), calls=%async_computation.3 | async-start | bytes 4194304 | tf_op jit(solution)/shard_map/all_to_all | solution.py:158
  458.1 220.8 %all-reduce.2.cloned.1.call-start = ((), (), s32[]{:S(2)}) async-start(), calls=%async_computation.8 | async-start | bytes 393216 | tf_op jit(solution)/shard_map/psum | solution.py:164
  530.7 149.7 %copy-start.7 = (f32[6,1,128,128]{2,3,1,0:T(8,128)S(1)}, f32[6,1,128,128]{2,3,1,0:T(8,128)}, u32[]{:S(2)}) copy-start(f32[6,1,128,128]{2,3,1,0:T(8,128)} %custom-call.28) | copy-start | bytes 1179652
  533.6 147.6 %copy-start.21 = (f32[6,128,128]{2,1,0:T(8,128)S(1)}, f32[6,128,128]{2,1,0:T(8,128)}, u32[]{:S(2)}) copy-start(f32[6,128,128]{2,1,0:T(8,128)} %fusion.52) | copy-start | bytes 1179652
  533.7 148.4 %copy-start.20 = (f32[6,128,128]{2,1,0:T(8,128)S(1)}, f32[6,128,128]{2,1,0:T(8,128)}, u32[]{:S(2)}) copy-start(f32[6,128,128]{2,1,0:T(8,128)} %copy-done.19) | copy-start | bytes 1179652
  533.7 149.4 %copy-start.31 = (pred[128,128]{1,0:T(8,128)(4,1)S(1)}, pred[128,128]{1,0:T(8,128)(4,1)}, u32[]{:S(2)}) copy-start(pred[128,128]{1,0:T(8,128)(4,1)} %copy-done.30) | copy-start | bytes 49156
  680.4 4.0 copy-start.27
  680.4 4.0 copy-start.35
  680.4 4.0 copy-start.38
  682.1 3.2 copy-start.18
  684.4 2.6 copy-start.32
  684.4 2.6 copy-start.33
  684.4 2.6 copy-start.34
  685.3 3.3 copy-start.29
  (5 other events, 5.0 us)
Sparse Core Ops, SparseCore 0:
  144.3 47.5 all-gather.2
  193.8 86.0 all-gather.4
  373.7 64.4 reduce-scatter.1
  529.4 149.4 all-reduce.1
where the time goes:
time: 709 us; the launch traced here: 698 us
  other arithmetic  238 us (34%)
  waiting for transfers between devices  202 us (28%)
  matrix products  119 us (17%)
  local copies, waits for them, and re-layouts  89.4 us (13%)
  starting transfers between devices  34.9 us (5%)
  between operations  15.3 us (2%)
    psum x1, waiting for transfers between devices, local(): owner_grad = lax.psum(block_share, 'seq').astype(jnp.float32)  143 us
    another operation x3, other arithmetic, cayley(): lax.linalg.triangular_solve(factor_low, halfway, left_side=True, lower=Tr...  120 us
    another operation x3, other arithmetic, cayley(): factor_low = jnp.linalg.cholesky(gram_matrix)  70.5 us
    gather x16, local copies, waits for them, and re-layouts, reorder(): jnp.take(matrix.reshape(row_count, ordering.shape[0], -1), ordering, axis=1)  38.8 us
    all_to_all x1, waiting for transfers between devices, local(): lax.all_to_all(local_rows, 'seq', split_axis=2, concat_axis=0, tiled=True)  35.6 us
    dot_general x1, matrix products, local(): lax.dot_general(upstream, weight_full, (((1,), (1,)), ((), ())), preferre...  17.7 us
    dot_general x4, matrix products, backward_block(): jnp.einsum('qhd,khd->hqk', dout_block, value_rows, preferred_element_type...  15.8 us
    all_to_all x1, waiting for transfers between devices, local(): lax.all_to_all(attended, 'seq', split_axis=0, concat_axis=1, tiled=True)  15.6 us
  transfers between devices with their start and end apart: 8, of which 5 were waited for; matrix products, arithmetic and copies ran while one was open for 33% of the time, Pallas kernels for 0%

commit v1 on v0

v1 whole, which is shorter than its diff:
```python
import functools
import math

import jax
import jax.numpy as jnp
from jax import lax
from jax.experimental import pallas as pl
from jax.experimental.pallas import tpu as pltpu
from jax.sharding import Mesh, PartitionSpec as P

HEADS = 16
HD = 128
BS = 128
FACTORS = 4
PIECE = 32
PER = BS // PIECE
BF = jnp.bfloat16
F32 = jnp.float32
HIGH = lax.Precision.HIGHEST
ROWS = ("xl", "y", "c")
SEQ = ("xh", "z")
QB = 256
LOG2E = 1.4426950408889634
MIB = 1024 * 1024


def params(limit, semantics=None):
    return pltpu.CompilerParams(vmem_limit_bytes=limit * MIB, dimension_semantics=semantics)


def inverse_kernel(skew_ref, inv_ref, rot_ref):
    count, size, _ = skew_ref.shape
    row = lax.broadcasted_iota(jnp.int32, (size, size), 0)
    col = lax.broadcasted_iota(jnp.int32, (size, size), 1)
    eye = (row == col).astype(F32)
    row8 = lax.broadcasted_iota(jnp.int32, (8, size), 0)
    col8 = lax.broadcasted_iota(jnp.int32, (8, size), 1)
    eye8 = (row8 == col8).astype(F32)
    rowp = lax.broadcasted_iota(jnp.int32, (size, 8), 0)
    colp = lax.broadcasted_iota(jnp.int32, (size, 8), 1)
    for b in range(count):
        params_b = skew_ref[b]
        inv_ref[b] = eye + params_b - params_b.T

    def step(g, carry):
        first = pl.multiple_of(g * 8, 8)
        panels = [inv_ref[b, pl.ds(first, 8), :] for b in range(count)]
        sides = [eye8] * count
        for j in range(8):
            pick = (lax.broadcasted_iota(jnp.int32, (8, 1), 0) == j).astype(F32)
            for b in range(count):
                panel, side = panels[b], sides[b]
                column = panel[:, j : j + 1]
                scale = 1.0 / panel[j : j + 1, j : j + 1]
                left = (column - pick) * scale
                panels[b] = panel - left * panel[j : j + 1, :]
                sides[b] = side - left * side[j : j + 1, :]
        selector = (rowp - first == colp).astype(F32)
        for b in range(count):
            whole = inv_ref[b]
            update = jnp.dot(
                whole[:, :8] - selector,
                panels[b] + sides[b],
                precision=HIGH,
                preferred_element_type=F32,
            )
            inv_ref[b] = pltpu.roll(whole - update, size - 8, 1)
        return carry

    lax.fori_loop(0, size // 8, step, 0)
    for b in range(count):
        rot_ref[b] = (2.0 * inv_ref[b] - eye).astype(BF)


def cayley(skew):
    return pl.pallas_call(
        inverse_kernel,
        out_shape=(
            jax.ShapeDtypeStruct(skew.shape, F32),
            jax.ShapeDtypeStruct(skew.shape, BF),
        ),
        compiler_params=params(32),
        name="cayley",
    )(skew)


def pullback_kernel(scaling, inv_ref, grad_ref, out_ref):
    for b in range(inv_ref.shape[0]):
        flipped = inv_ref[b].T
        grad = grad_ref[b].astype(F32) * (-2.0 * scaling)
        inner = jnp.dot(flipped, grad, precision=HIGH, preferred_element_type=F32)
        grad_s = jnp.dot(inner, flipped, precision=HIGH, preferred_element_type=F32)
        out_ref[b] = grad_s - grad_s.T


def cayley_pullback(inverse, grad, scaling):
    return pl.pallas_call(
        functools.partial(pullback_kernel, scaling),
        out_shape=jax.ShapeDtypeStruct(inverse.shape, F32),
        compiler_params=params(32),
        name="cayley_pullback",
    )(inverse, grad)


def attend_kernel(q_ref, k_ref, v_ref, att_ref, wide_ref, exps_ref, sums_ref, vt_ref):
    @pl.when(pl.program_id(0) == 0)
    def _():
        vt_ref[...] = v_ref[...].reshape(-1, HD).T

    queries = q_ref[...].reshape(QB, HD)
    keys = k_ref[...].reshape(-1, HD)
    scores = lax.dot_general(keys, queries, (((1,), (1,)), ((), ())), preferred_element_type=F32)
    factor = LOG2E / math.sqrt(HD)
    top = jnp.max(scores, axis=0, keepdims=True)
    exps = jnp.exp2((scores - top) * factor)
    total = jnp.sum(exps, axis=0, keepdims=True)
    low = exps.astype(BF)
    exps_ref[0] = low
    wide = jnp.dot(vt_ref[...], low, preferred_element_type=F32) / total
    wide_ref[0] = wide
    sums_ref[0] = 1.0 / total
    att_ref[...] = wide.T.astype(BF).reshape(att_ref.shape)


def attend(spread):
    groups, _, tok, _ = spread.shape
    length = groups * tok
    per = QB // tok
    steps = length // QB
    return pl.pallas_call(
        attend_kernel,
        grid=(steps,),
        in_specs=[
            pl.BlockSpec((per, 1, tok, HD), lambda i: (i, 0, 0, 0)),
            pl.BlockSpec((groups, 1, tok, HD), lambda i: (0, 1, 0, 0)),
            pl.BlockSpec((groups, 1, tok, HD), lambda i: (0, 2, 0, 0)),
        ],
        out_specs=[
            pl.BlockSpec((per, tok, HD), lambda i: (i, 0, 0)),
            pl.BlockSpec((1, HD, QB), lambda i: (i, 0, 0)),
            pl.BlockSpec((1, length, QB), lambda i: (i, 0, 0)),
            pl.BlockSpec((1, 1, QB), lambda i: (i, 0, 0)),
        ],
        out_shape=[
            jax.ShapeDtypeStruct((groups, tok, HD), BF),
            jax.ShapeDtypeStruct((steps, HD, QB), F32),
            jax.ShapeDtypeStruct((steps, length, QB), BF),
            jax.ShapeDtypeStruct((steps, 1, QB), F32),
        ],
        scratch_shapes=[pltpu.VMEM((HD, length), BF)],
        compiler_params=params(58, ("arbitrary",)),
        cost_estimate=pl.CostEstimate(
            flops=4 * length * length * HD, bytes_accessed=2 * length * length, transcendentals=length * length
        ),
        name="attend",
    )(spread, spread, spread)


def attend_back_kernel(
    q_ref, k_ref, v_ref, dout_ref, wide_ref, exps_ref, sums_ref, out_ref, kt_ref, dk_ref, dv_ref
):
    step = pl.program_id(0)
    groups, _, tok, _ = k_ref.shape
    per = QB // tok

    @pl.when(step == 0)
    def _():
        kt_ref[...] = k_ref[...].reshape(-1, HD).T
        dk_ref[...] = jnp.zeros_like(dk_ref)
        dv_ref[...] = jnp.zeros_like(dv_ref)

    queries = q_ref[...].reshape(QB, HD)
    values = v_ref[...].reshape(-1, HD)
    dout = jnp.concatenate([dout_ref[p] for p in range(per)], axis=1)
    inv_sum = sums_ref[0]
    wide_dout = dout.astype(F32)
    low = exps_ref[0]
    dv_ref[...] += lax.dot_general(
        low, (wide_dout * inv_sum).astype(BF), (((1,), (1,)), ((), ())), preferred_element_type=F32
    )
    centre = jnp.sum(wide_dout * wide_ref[0], axis=0, keepdims=True)
    dprobs = jnp.dot(values, dout, preferred_element_type=F32)
    dscores = (low.astype(F32) * ((dprobs - centre) * (inv_sum * (1.0 / math.sqrt(HD))))).astype(BF)
    dk_ref[...] += jnp.dot(dscores, queries, preferred_element_type=F32)
    dq = jnp.dot(kt_ref[...], dscores, preferred_element_type=F32)
    out_ref[pl.ds(step * per, per), 0] = dq.T.astype(BF).reshape(per, tok, HD)

    @pl.when(step == pl.num_programs(0) - 1)
    def _():
        out_ref[:, 1] = dk_ref[...].astype(BF).reshape(groups, tok, HD)
        out_ref[:, 2] = dv_ref[...].astype(BF).reshape(groups, tok, HD)


def attend_back(spread, dout, wide, exps, sums):
    groups, _, tok, _ = spread.shape
    length = groups * tok
    per = QB // tok
    steps = length // QB
    return pl.pallas_call(
        attend_back_kernel,
        grid=(steps,),
        in_specs=[
            pl.BlockSpec((per, 1, tok, HD), lambda i: (i, 0, 0, 0)),
            pl.BlockSpec((groups, 1, tok, HD), lambda i: (0, 1, 0, 0)),
            pl.BlockSpec((groups, 1, tok, HD), lambda i: (0, 2, 0, 0)),
            pl.BlockSpec((per, HD, tok), lambda i: (i, 0, 0)),
            pl.BlockSpec((1, HD, QB), lambda i: (i, 0, 0)),
            pl.BlockSpec((1, length, QB), lambda i: (i, 0, 0)),
            pl.BlockSpec((1, 1, QB), lambda i: (i, 0, 0)),
        ],
        out_specs=pl.BlockSpec((groups, 3, tok, HD), lambda i: (0, 0, 0, 0)),
        out_shape=jax.ShapeDtypeStruct((groups, 3, tok, HD), BF),
        scratch_shapes=[
            pltpu.VMEM((HD, length), BF),
            pltpu.VMEM((length, HD), F32),
            pltpu.VMEM((length, HD), F32),
        ],
        compiler_params=params(58, ("arbitrary",)),
        cost_estimate=pl.CostEstimate(
            flops=8 * length * length * HD, bytes_accessed=2 * length * length, transcendentals=0
        ),
        name="attend_back",
    )(spread, spread, spread, dout, wide, exps, sums)


def gather_block(order_ref, factor, j, source_ref):
    pieces = []
    for p in range(PER):
        at = pl.multiple_of(order_ref[factor, j * PER + p] * PIECE, PIECE)
        pieces.append(source_ref[pl.ds(at, PIECE), :])
    return jnp.concatenate(pieces, axis=0)


def scatter_block(order_ref, factor, j, block, target_ref):
    for p in range(PER):
        at = pl.multiple_of(order_ref[factor, j * PER + p] * PIECE, PIECE)
        target_ref[pl.ds(at, PIECE), :] = block[p * PIECE : (p + 1) * PIECE, :]


def down_kernel(order_ref, home_ref, cot_ref, near_ref, far_ref, moved_ref, up_ref, flip_ref, rot_ref, a_ref, b_ref):
    blocks = cot_ref.shape[1] // BS
    half = near_ref.shape[0]

    def place(i, carry):
        for base, source in ((0, near_ref), (half, far_ref)):
            rot = source[i]
            at = home_ref[base + i]
            rot_ref[at] = rot
            flip_ref[at] = rot.T
        return carry

    lax.fori_loop(0, half, place, 0, unroll=4)
    for j in range(blocks):
        a_ref[j * BS : (j + 1) * BS, :] = cot_ref[:, j * BS : (j + 1) * BS].T
    source, target = a_ref, b_ref
    for factor in reversed(range(FACTORS)):
        if factor == 0:
            target = up_ref

        def body(j, carry, factor=factor, source=source, target=target):
            block = gather_block(order_ref, factor, j, source)
            moved_ref[factor, pl.ds(pl.multiple_of(j * BS, BS), BS), :] = block
            back = jnp.dot(
                rot_ref[factor * blocks + j], block, preferred_element_type=F32
            ).astype(BF)
            scatter_block(order_ref, factor, j, back, target)
            return carry

        lax.fori_loop(0, blocks, body, 0, unroll=4)
        source, target = target, source


def down(orders, home, cotangent, near, far):
    tok, width = cotangent.shape
    total = 2 * near.shape[0]
    smem = pl.BlockSpec(memory_space=pltpu.SMEM)
    vmem = pl.BlockSpec(memory_space=pltpu.VMEM)
    return pl.pallas_call(
        down_kernel,
        in_specs=[smem, smem, vmem, vmem, vmem],
        out_specs=[vmem, vmem, vmem],
        out_shape=[
            jax.ShapeDtypeStruct((FACTORS, width, tok), BF),
            jax.ShapeDtypeStruct((width, tok), BF),
            jax.ShapeDtypeStruct((total, BS, BS), BF),
        ],
        scratch_shapes=[
            pltpu.VMEM((total, BS, BS), BF),
            pltpu.VMEM((width, tok), BF),
            pltpu.VMEM((width, tok), BF),
        ],
        compiler_params=params(40),
        cost_estimate=pl.CostEstimate(flops=10**9, bytes_accessed=10**7, transcendentals=0),
        name="butterfly_down",
    )(orders, home, cotangent, near, far)


def up_kernel(order_ref, self_ref, proj_ref, flip_ref, moved_ref, out_ref, mine_ref, other_ref, a_ref, b_ref):
    blocks = proj_ref.shape[1] // BS
    owned = mine_ref.shape[1]
    xl, y, core = self_ref[0], self_ref[1], self_ref[2]
    for j in range(blocks):
        a_ref[j * BS : (j + 1) * BS, :] = proj_ref[:, j * BS : (j + 1) * BS].T
    source, target = a_ref, b_ref
    for factor in range(FACTORS):
        for half, grad_ref in ((core, mine_ref), (1 - core, other_ref)):

            def body(i, carry, factor=factor, source=source, target=target, half=half, grad_ref=grad_ref):
                pair, inside = i // owned, i % owned
                j = (2 * pair + half) * owned + inside
                at = factor * blocks + j
                block = gather_block(order_ref, factor, j, source)
                mixed = jnp.dot(flip_ref[at], block, preferred_element_type=F32).astype(BF)
                scatter_block(order_ref, factor, j, mixed, target)
                moved = moved_ref[factor, pl.ds(pl.multiple_of(j * BS, BS), BS), :]
                owner = factor * (blocks // (2 * owned)) + pair
                slot = ((owner // 4) ^ xl) * 4 + ((owner % 4 + 4 - y) % 4)
                grad_ref[slot, inside] = lax.dot_general(
                    block, moved, (((1,), (1,)), ((), ())), preferred_element_type=F32
                ).astype(BF)
                return carry

            lax.fori_loop(0, blocks // 2, body, 0, unroll=4)
        source, target = target, source
    for j in range(blocks):
        out_ref[:, j * BS : (j + 1) * BS] = source[j * BS : (j + 1) * BS, :].T


def up(orders, position, projected, flipped, moved):
    tok, width = projected.shape
    smem = pl.BlockSpec(memory_space=pltpu.SMEM)
    vmem = pl.BlockSpec(memory_space=pltpu.VMEM)
    owned = flipped.shape[0] // 16
    half = jax.ShapeDtypeStruct((8, owned, BS, BS), BF)
    return pl.pallas_call(
        up_kernel,
        in_specs=[smem, smem, vmem, vmem, vmem],
        out_specs=[vmem, vmem, vmem],
        out_shape=[jax.ShapeDtypeStruct((tok, width), BF), half, half],
        scratch_shapes=[pltpu.VMEM((width, tok), BF), pltpu.VMEM((width, tok), BF)],
        compiler_params=params(40),
        cost_estimate=pl.CostEstimate(flops=10**9, bytes_accessed=10**7, transcendentals=0),
        name="butterfly_up",
    )(orders, position, projected, flipped, moved)


def products_kernel(weight_ref, up_ref, att_ref, back_ref, proj_ref, acc_ref):
    step = pl.program_id(0)
    weight = weight_ref[...]
    back_ref[...] = jnp.dot(weight, up_ref[...], preferred_element_type=F32).astype(BF)
    att = jnp.concatenate([att_ref[p] for p in range(att_ref.shape[0])], axis=1)
    term = jnp.dot(att, weight, preferred_element_type=F32)

    @pl.when(step == 0)
    def _():
        acc_ref[...] = term

    @pl.when(step > 0)
    def _():
        acc_ref[...] += term

    @pl.when(step == pl.num_programs(0) - 1)
    def _():
        proj_ref[...] = acc_ref[...].astype(BF)


def products(weight, upstream, att):
    rows, width = weight.shape
    tok = upstream.shape[1]
    tile = 256
    return pl.pallas_call(
        products_kernel,
        grid=(rows // tile,),
        in_specs=[
            pl.BlockSpec((tile, width), lambda i: (i, 0)),
            pl.BlockSpec((width, tok), lambda i: (0, 0)),
            pl.BlockSpec((tile // HD, tok, HD), lambda i: (i, 0, 0)),
        ],
        out_specs=[
            pl.BlockSpec((tile, tok), lambda i: (i, 0)),
            pl.BlockSpec((tok, width), lambda i: (0, 0)),
        ],
        out_shape=[
            jax.ShapeDtypeStruct((rows, tok), BF),
            jax.ShapeDtypeStruct((tok, width), BF),
        ],
        scratch_shapes=[pltpu.VMEM((tok, width), F32)],
        compiler_params=params(58, ("arbitrary",)),
        cost_estimate=pl.CostEstimate(
            flops=4 * rows * width * tok, bytes_accessed=2 * rows * width, transcendentals=0
        ),
        name="products",
    )(weight, upstream, att)


def swap(x, axis):
    return lax.ppermute(x, axis, [(0, 1), (1, 0)])


def shift(x, axis, by):
    n = lax.axis_size(axis)
    return lax.ppermute(x, axis, [(i, (i + by) % n) for i in range(n)])


def turn(x, by):
    order = [(x_hi * 2 + x_lo) for x_lo in range(2) for x_hi in range(2)]
    at = {x: i for i, x in enumerate(order)}
    return lax.ppermute(x, ("xl", "xh"), [(at[i], at[(i + by) % 4]) for i in range(4)])


def cross(x):
    half = x.shape[0] // 2
    return jnp.concatenate([turn(x[:half], 1), turn(x[half:], 3)], axis=0)


def partner(x, axis, bit):
    return lax.ppermute(x, axis, [(i, i ^ bit) for i in range(lax.axis_size(axis))])


def add(*terms):
    return sum(t.astype(F32) for t in terms).astype(BF)


def after(x, *others):
    return lax.optimization_barrier((x,) + others)[0]


def gather_column(own):
    return jnp.concatenate([own, shift(own, "y", 1), shift(own, "y", 3), shift(own, "y", 2)], axis=0)


def gather_blocks(column, earlier):
    count = column.shape[0] // 4
    near = jnp.concatenate([column, after(cross(column), earlier)], axis=0)
    far = swap(near, "c")
    at = jnp.arange(16 * count, dtype=jnp.int32)
    slot, inside = at // count, at % count
    back = jnp.array([0, 1, 3, 2], jnp.int32)[slot % 4]
    y = (lax.axis_index("y") - back) % 4
    xl = lax.axis_index("xl") ^ ((slot // 4) % 2)
    c = lax.axis_index("c") ^ (slot // 8)
    return near, far, ((xl * 4 + y) * 2 + c) * count + inside


def local(attn_inputs, out_weight, skew_params, piece_orders, cotangent):
    tok = attn_inputs.shape[1]
    width = out_weight.shape[1]
    seqs = 16
    position = jnp.stack([lax.axis_index(a) for a in ROWS]).astype(jnp.int32)
    weight = lax.all_gather(out_weight, ROWS, axis=0, tiled=True)
    rows = attn_inputs[0].reshape(tok, 3, seqs, HD).transpose(2, 1, 0, 3)
    spread = lax.all_to_all(rows, SEQ, split_axis=0, concat_axis=0, tiled=True)
    inverse, rot_own = cayley(after(skew_params, rows))
    column = gather_column(rot_own)
    spread, column = lax.optimization_barrier((spread, column))
    att, wide, exps, sums = attend(spread)
    att_own = lax.all_to_all(att, SEQ, split_axis=0, concat_axis=0, tiled=True)
    near, far, home = gather_blocks(column, att_own)
    moved_grad, upstream, flipped = down(piece_orders, home, cotangent[0], near, far)
    grad_att, projected = products(weight, upstream, att_own)
    dout = lax.all_to_all(
        grad_att.reshape(seqs, HD, tok), SEQ, split_axis=0, concat_axis=0, tiled=True
    )
    block_output, mine, other = up(piece_orders, position, projected, flipped, moved_grad)
    mine, other, dout = lax.optimization_barrier((mine, other, dout))
    from_core = swap(other, "c")
    send = add(mine[4:], from_core[4:])
    from_xl = cross(send)
    grads = attend_back(spread, after(dout, send), wide, exps, sums)
    from_xl, grads = lax.optimization_barrier((from_xl, grads))
    grads = lax.all_to_all(grads, SEQ, split_axis=0, concat_axis=0, tiled=True)
    grad_inputs = grads.transpose(2, 1, 0, 3).reshape(1, tok, 3, seqs * HD)
    share = add(mine[:4], from_core[:4], from_xl)
    owner_grad = add(share[0], *[shift(share[dy], "y", dy) for dy in (2, 1, 3)])
    for axis, bit in (("xh", 1), ("z", 1), ("z", 2), ("z", 4)):
        owner_grad = add(owner_grad, partner(owner_grad, axis, bit))
    total_tokens = 16 * tok * seqs
    grad_skew = cayley_pullback(inverse, owner_grad, 1.0 / math.sqrt(total_tokens))
    return block_output[None], grad_inputs, grad_skew


def solution(mesh):
    fine = Mesh(mesh.devices.reshape(2, 4, 2, 2, 8), ROWS + SEQ)
    in_specs = (
        P(ROWS, SEQ, None, None),
        P(ROWS, None),
        P(ROWS, None, None),
        P(),
        P(ROWS, SEQ, None),
    )
    out_specs = (P(ROWS, SEQ, None), P(ROWS, SEQ, None, None), P(ROWS, None, None))
    return jax.shard_map(local, mesh=fine, in_specs=in_specs, out_specs=out_specs, check_vma=False)
```

time: 709 us -> 279 us (0.39); the launches traced: 698 us -> 278 us
  other arithmetic: 238 us -> 5.23 us
  matrix products: 119 us -> 0 us
  waiting for transfers between devices: 202 us -> 94.9 us
  Pallas kernels: 0 us -> 80.8 us
  local copies, waits for them, and re-layouts: 89.4 us -> 18.9 us
  starting transfers between devices: 34.9 us -> 63.5 us
    another operation x7 -> x1, other arithmetic: 193 us -> 0.08 us  [local(): position = jnp.stack([lax.axis_index(a) for a in ROWS]).astype(jnp.int32)]
    psum x1 -> x0, waiting for transfers between devices: 143 us -> none  [local(): owner_grad = lax.psum(block_share, 'seq').astype(jnp.float32)]
    dot_general x47 -> x0, matrix products: 109 us -> none  [the longest x1 17.7 us: local(): lax.dot_general(upstream, weight_full, (((1,), (1,)), ((), ())), preferre...]
    ppermute x0 -> x16, waiting for transfers between devices: none -> 91.7 us  [the longest x4 37.1 us: partner(): lax.ppermute(x, axis, [(i, i ^ bit) for i in range(lax.axis_size(axis))])]
    pallas_call x0 -> x7, Pallas kernels: none -> 80.8 us  [the longest x1 21.2 us: cayley(): pl.pallas_call(inverse_kernel, out_shape=(jax.ShapeDtypeStruct(skew.shape...]
    all_to_all x4, waiting for transfers between devices: 51.2 us -> 2.54 us  [the longest x1 2.53 us: local(): lax.all_to_all(grad_att.reshape(seqs, HD, tok), SEQ, split_axis=0, concat...]
    gather x16 -> x0, local copies, waits for them, and re-layouts: 38.8 us -> none  [reorder(): jnp.take(matrix.reshape(row_count, ordering.shape[0], -1), ordering, axis=1)]
    ppermute x0 -> x16, starting transfers between devices: none -> 27.1 us  [the longest x4 15 us: partner(): lax.ppermute(x, axis, [(i, i ^ bit) for i in range(lax.axis_size(axis))])]
  transfers between devices with their start and end apart: 8 -> 21, of which waited for: 5 -> 13; matrix products, arithmetic and copies ran while one was open for 33% -> 2% of each run, Pallas kernels for 0% -> 25%
where the time goes in v1:
time: 279 us; the launch traced here: 278 us
  waiting for transfers between devices  94.9 us (34%)
  Pallas kernels  80.8 us (29%)
  starting transfers between devices  63.5 us (23%)
  local copies, waits for them, and re-layouts  18.9 us (7%)
  between operations  14.3 us (5%)
  other arithmetic  5.23 us (2%)
    ppermute x4, waiting for transfers between devices, partner(): lax.ppermute(x, axis, [(i, i ^ bit) for i in range(lax.axis_size(axis))])  37.1 us
    ppermute x6, waiting for transfers between devices, shift(): return lax.ppermute(x, axis, [(i, (i + by) % n) for i in range(n)])  27.5 us
    pallas_call x1, Pallas kernels, cayley(): pl.pallas_call(inverse_kernel, out_shape=(jax.ShapeDtypeStruct(skew.shape...  21.2 us
    ppermute x4, waiting for transfers between devices, turn(): lax.ppermute(x, ('xl', 'xh'), [(at[i], at[(i + by) % 4]) for i in range(4)])  20.1 us
    unnamed x33, local copies, waits for them, and re-layouts  16.2 us
    ppermute x4, starting transfers between devices, partner(): lax.ppermute(x, axis, [(i, i ^ bit) for i in range(lax.axis_size(axis))])  15 us
    pallas_call x1, Pallas kernels, attend_back(): pl.pallas_call(attend_back_kernel, grid=(steps,), in_specs=[pl.BlockSpec(...  14.5 us
    pallas_call x1, Pallas kernels, attend(): pl.pallas_call(attend_kernel, grid=(steps,), in_specs=[pl.BlockSpec((per,...  14.4 us
  transfers between devices with their start and end apart: 21, of which 13 were waited for; matrix products, arithmetic and copies ran while one was open for 2% of the time, Pallas kernels for 25%

profile of v1, /device:TPU:24, one launch (start us, length us, event | category | flops | bytes accessed | tf_op | source)
XLA Modules:
  0.0 277.7 jit_solution(4665871260086116951)
XLA Ops:
  7.9 1.9 copy.9
  9.8 1.6 copy.10
  11.4 11.2 %all-to-all-start = ((bf16[16,3,128,128]{3,2,1,0:T(8,128)(2,1)}), bf16[16,3,128,128]{3,2,1,0:T(8,128)(2,1)S(1)}, u32[]{:S(2)}, u32[]{:S(2)}) async-start(bf16[16,3,128,128]{3,2,1,0:T(8,128)(2,1)} %bitcast.35), calls=%async_computation | async-start | bytes 3145728 | tf_op jit(solution)/shard_map/all_to_all | solution.py:452
  22.6 21.2 %cayley.1 = (f32[6,128,128]{2,1,0:T(8,128)S(1)}, bf16[6,128,128]{2,1,0:T(8,128)(2,1)S(1)}) custom-call(f32[6,128,128]{2,1,0:T(8,128)S(1)} %copy-done.9), custom_call_target="tpu_custom_call" | custom-call | tf_op jit(solution)/shard_map/cayley/pallas_call | solution.py:76
  44.1 1.8 collective-permute-start.1
  45.9 1.2 collective-permute-start.2
  47.1 8.7 %collective-permute-done = bf16[6,128,128]{2,1,0:T(8,128)(2,1)S(1)} collective-permute-done((bf16[6,128,128]{2,1,0:T(8,128)(2,1)S(1)}, bf16[6,128,128]{2,1,0:T(8,128)(2,1)S(1)}, u32[]{:S(2)}, u32[]{:S(2)}) %collective-permute-start) | collective-permute-done | bytes 196640 | tf_op jit(solution)/shard_map/ppermute | solution.py:402
  55.8 9.1 %collective-permute-done.2 = bf16[6,128,128]{2,1,0:T(8,128)(2,1)S(1)} collective-permute-done((bf16[6,128,128]{2,1,0:T(8,128)(2,1)S(1)}, bf16[6,128,128]{2,1,0:T(8,128)(2,1)S(1)}, u32[]{:S(2)}, u32[]{:S(2)}) %collective-permute-start.2) | collective-permute-done | bytes 196640 | tf_op jit(solution)/shard_map/ppermute | solution.py:402
  65.0 1.1 copy-done.12
  66.2 14.4 %attend.1 = (bf16[16,128,128]{2,1,0:T(8,128)(2,1)}, f32[8,128,256]{2,1,0:T(8,128)}, bf16[8,2048,256]{2,1,0:T(8,128)(2,1)}, f32[8,1,256]{2,1,0:T(1,128)}) custom-call(bf16[16,3,128,128]{3,2,1,0:T(8,128)(2,1)} %copy-done.12, bf16[16,3,128,128]{3,2,1,0:T(8,128)(2,1)} %copy-done.12, bf16[16,3,128,128]{3,2,1,0:T(8,128)(2,1)} %copy-done.12), custom_call_target="tpu_custom_call" | custom-call | flops 2147483648 | bytes 8388608 | tf_op jit(solution)/shard_map/attend/pallas_call | solution.py:130
  80.6 9.5 %all-to-all-start.1 = ((bf16[16,128,128]{2,1,0:T(8,128)(2,1)}), bf16[16,128,128]{2,1,0:T(8,128)(2,1)S(1)}, u32[]{:S(2)}, u32[]{:S(2)}) async-start(bf16[16,128,128]{2,1,0:T(8,128)(2,1)} %get-tuple-element.31), calls=%async_computation.1 | async-start | bytes 1048576 | tf_op jit(solution)/shard_map/all_to_all | solution.py:457
  90.2 3.2 %collective-permute-start.4 = (bf16[12,128,128]{2,1,0:T(8,128)(2,1)S(1)}, bf16[12,128,128]{2,1,0:T(8,128)(2,1)S(1)}, u32[]{:S(2)}, u32[]{:S(2)}) collective-permute-start(bf16[12,128,128]{2,1,0:T(8,128)(2,1)S(1)} %get-tuple-element.60), channel_id=1, source_target_pairs={{0,136},{128,0},{8,128},{136,8},{1,137},{129,1},{9,129},{137,9},{2... | collective-permute-start | bytes 1179656 | tf_op jit(solution)/shard_map/ppermute | solution.py:408
  93.5 19.1 %collective-permute-done.3 = bf16[12,128,128]{2,1,0:T(8,128)(2,1)S(1)} collective-permute-done((bf16[12,128,128]{2,1,0:T(8,128)(2,1)S(1)}, bf16[12,128,128]{2,1,0:T(8,128)(2,1)S(1)}, u32[]{:S(2)}, u32[]{:S(2)}) %collective-permute-start.3) | collective-permute-done | bytes 393248 | tf_op jit(solution)/shard_map/ppermute | solution.py:408
  112.6 1.0 collective-permute-done.4
  114.7 3.4 %collective-permute-done.5.far_ref = bf16[48,128,128]{2,1,0:T(8,128)(2,1)S(1)} collective-permute-done((bf16[48,128,128]{2,1,0:T(8,128)(2,1)S(1)}, bf16[48,128,128]{2,1,0:T(8,128)(2,1)S(1)}, u32[]{:S(2)}, u32[]{:S(2)}) %collective-permute-start.5) | collective-permute-done | bytes 1572896 | tf_op jit(solution)/shard_map/ppermute | solution.py:397
  118.1 1.1 copy-done.6
  119.2 7.5 %butterfly_down.1 = (bf16[4,3072,128]{2,1,0:T(8,128)(2,1)S(1)}, bf16[3072,128]{1,0:T(8,128)(2,1)S(1)}, bf16[96,128,128]{2,1,0:T(8,128)(2,1)S(1)}) custom-call(s32[4,96]{1,0:T(4,128)S(1)} %copy-done.10, s32[96]{0:T(128)S(1)} %fusion.3.home_ref, bf16[128,3072]{1,0:T(8,128)(2,1)S(1)} %bitcast.33, ...), custom_call_target="tpu_custom_call" | custom-call | flops 1000000000 | bytes 10000000 | tf_op jit(solution)/shard_map/butterfly_down/pallas_call | solution.py:278
  126.7 1.7 copy-done
  128.5 1.6 copy-done.2
  131.0 12.0 %products.1 = (bf16[2048,128]{1,0:T(8,128)(2,1)}, bf16[128,3072]{1,0:T(8,128)(2,1)}) custom-call(bf16[2048,3072]{1,0:T(8,128)(2,1)} %all-gather.2.cloned.1.call-done.weight_ref, bf16[3072,128]{1,0:T(8,128)(2,1)} %copy-done.8, bf16[16,128,128]{2,1,0:T(8,128)(2,1)} %copy-done.13), custom_call_target="tpu_custom_call" | custom-call | flops 3221225472 | bytes 12582912 | tf_op jit(solution)/shard_map/products/pallas_call | solution.py:371
  143.0 9.7 %all-to-all-start.2 = ((bf16[16,128,128]{2,1,0:T(8,128)(2,1)}), bf16[16,128,128]{2,1,0:T(8,128)(2,1)}, u32[]{:S(2)}, u32[]{:S(2)}) async-start(bf16[16,128,128]{2,1,0:T(8,128)(2,1)} %bitcast.38), calls=%async_computation.2 | async-start | bytes 1048576 | tf_op jit(solution)/shard_map/all_to_all | solution.py:461
  152.8 1.9 copy-done.3
  154.7 1.1 copy-done.7
  155.8 9.3 %butterfly_up.1 = (bf16[128,3072]{1,0:T(8,128)(2,1)}, bf16[8,6,128,128]{3,2,1,0:T(8,128)(2,1)S(1)}, bf16[8,6,128,128]{3,2,1,0:T(8,128)(2,1)S(1)}) custom-call(s32[4,96]{1,0:T(4,128)S(1)} %copy-done.10, s32[3]{0:T(128)S(1)} %pad_add_fusion.self_ref, bf16[128,3072]{1,0:T(8,128)(2,1)S(1)} %copy-done.7, bf16[96,128,128]{2,1,0:T(8,128)(2,1)S(1)} %copy-done.3, ...), custom_call_target="tpu_custom_call" | custom-call | flops 1000000000 | bytes 10000000 | tf_op jit(solution)/shard_map/butterfly_up/pallas_call | solution.py:335
  165.1 1.2 copy-done.4
  166.3 1.2 copy-done.11
  167.5 2.5 all-to-all-done.2.dout_ref
  170.0 3.6 %collective-permute-done.6 = bf16[8,6,128,128]{3,2,1,0:T(8,128)(2,1)S(1)} collective-permute-done((bf16[8,6,128,128]{3,2,1,0:T(8,128)(2,1)}, bf16[8,6,128,128]{3,2,1,0:T(8,128)(2,1)S(1)}, u32[]{:S(2)}, u32[]{:S(2)}) %collective-permute-start.6) | collective-permute-done | bytes 1572896 | tf_op jit(solution)/shard_map/ppermute | solution.py:397
  173.6 1.9 add_convert_fusion.1
  176.2 2.7 collective-permute-start.8
  178.9 14.5 %attend_back.1 = bf16[16,3,128,128]{3,2,1,0:T(8,128)(2,1)} custom-call(bf16[16,3,128,128]{3,2,1,0:T(8,128)(2,1)} %copy-done.12, bf16[16,3,128,128]{3,2,1,0:T(8,128)(2,1)} %copy-done.12, bf16[16,3,128,128]{3,2,1,0:T(8,128)(2,1)} %copy-done.12, bf16[16,128,128]{2,1,0:T(8,128)(2,1)} %all-to-all-done.2.dout_ref, f32[8,128,256]{2,1,0:T(8,128)} %get-tuple-element.45.wide_ref, ...), custom_call_target="tpu_custom_call" | custom-call | flops 4294967296 | bytes 8388608 | tf_op jit(solution)/shard_map/attend_back/pallas_call | solution.py:199
  193.5 0.9 pad_maximum_fusion.2
  194.5 6.0 %all-to-all-start.3 = ((bf16[16,3,128,128]{3,2,1,0:T(8,128)(2,1)}), bf16[16,3,128,128]{3,2,1,0:T(8,128)(2,1)S(1)}, u32[]{:S(2)}, u32[]{:S(2)}) async-start(bf16[16,3,128,128]{3,2,1,0:T(8,128)(2,1)} %attend_back.1), calls=%async_computation.3 | async-start | bytes 3145728 | tf_op jit(solution)/shard_map/all_to_all | solution.py:471
  200.4 1.8 add_convert_fusion
  202.8 1.5 collective-permute-start.11
  204.4 5.8 %collective-permute-done.10 = bf16[6,128,128]{2,1,0:T(8,128)(2,1)S(1)} collective-permute-done((bf16[6,128,128]{2,1,0:T(8,128)(2,1)S(1)}, bf16[6,128,128]{2,1,0:T(8,128)(2,1)S(1)}, u32[]{:S(2)}, u32[]{:S(2)}) %collective-permute-start.10) | collective-permute-done | bytes 196640 | tf_op jit(solution)/shard_map/ppermute | solution.py:402
  210.2 3.9 %collective-permute-done.11 = bf16[6,128,128]{2,1,0:T(8,128)(2,1)S(1)} collective-permute-done((bf16[6,128,128]{2,1,0:T(8,128)(2,1)S(1)}, bf16[6,128,128]{2,1,0:T(8,128)(2,1)S(1)}, u32[]{:S(2)}, u32[]{:S(2)}) %collective-permute-start.11) | collective-permute-done | bytes 196640 | tf_op jit(solution)/shard_map/ppermute | solution.py:402
  214.2 3.2 %collective-permute-start.12 = (bf16[6,128,128]{2,1,0:T(8,128)(2,1)S(1)}, bf16[6,128,128]{2,1,0:T(8,128)(2,1)S(1)}, u32[]{:S(2)}, u32[]{:S(2)}) collective-permute-start(bf16[6,128,128]{2,1,0:T(8,128)(2,1)S(1)} %fusion.2), channel_id=1, source_target_pairs={{0,8},{8,0},{1,9},{9,1},{2,10},{10,2},{3,11},{11,3},{4,12},{12,4},... | collective-permute-start | bytes 589832 | tf_op jit(solution)/shard_map/ppermute | solution.py:417
  217.4 6.5 %collective-permute-done.12 = bf16[6,128,128]{2,1,0:T(8,128)(2,1)S(1)} collective-permute-done((bf16[6,128,128]{2,1,0:T(8,128)(2,1)S(1)}, bf16[6,128,128]{2,1,0:T(8,128)(2,1)S(1)}, u32[]{:S(2)}, u32[]{:S(2)}) %collective-permute-start.12) | collective-permute-done | bytes 196640 | tf_op jit(solution)/shard_map/ppermute | solution.py:417
  223.9 4.0 %collective-permute-start.13 = (bf16[6,128,128]{2,1,0:T(8,128)(2,1)S(1)}, bf16[6,128,128]{2,1,0:T(8,128)(2,1)S(1)}, u32[]{:S(2)}, u32[]{:S(2)}) collective-permute-start(bf16[6,128,128]{2,1,0:T(8,128)(2,1)S(1)} %add_convert_fusion.5), channel_id=1, source_target_pairs={{0,1},{1,0},{2,3},{3,2},{4,5},{5,4},{6,7},{7,6},{8,9},{9,8},{10,11... | collective-permute-start | bytes 589832 | tf_op jit(solution)/shard_map/ppermute | solution.py:417
  228.0 12.4 %collective-permute-done.13 = bf16[6,128,128]{2,1,0:T(8,128)(2,1)S(1)} collective-permute-done((bf16[6,128,128]{2,1,0:T(8,128)(2,1)S(1)}, bf16[6,128,128]{2,1,0:T(8,128)(2,1)S(1)}, u32[]{:S(2)}, u32[]{:S(2)}) %collective-permute-start.13) | collective-permute-done | bytes 196640 | tf_op jit(solution)/shard_map/ppermute | solution.py:417
  240.4 2.6 collective-permute-start.14
  243.0 8.3 %collective-permute-done.14 = bf16[6,128,128]{2,1,0:T(8,128)(2,1)S(1)} collective-permute-done((bf16[6,128,128]{2,1,0:T(8,128)(2,1)S(1)}, bf16[6,128,128]{2,1,0:T(8,128)(2,1)S(1)}, u32[]{:S(2)}, u32[]{:S(2)}) %collective-permute-start.14) | collective-permute-done | bytes 196640 | tf_op jit(solution)/shard_map/ppermute | solution.py:417
  251.3 5.1 %collective-permute-start.15 = (bf16[6,128,128]{2,1,0:T(8,128)(2,1)S(1)}, bf16[6,128,128]{2,1,0:T(8,128)(2,1)S(1)}, u32[]{:S(2)}, u32[]{:S(2)}) collective-permute-start(bf16[6,128,128]{2,1,0:T(8,128)(2,1)S(1)} %add_convert_fusion.3), channel_id=1, source_target_pairs={{0,4},{1,5},{2,6},{3,7},{4,0},{5,1},{6,2},{7,3},{8,12},{9,13},{10,... | collective-permute-start | bytes 589832 | tf_op jit(solution)/shard_map/ppermute | solution.py:417
  256.4 10.0 %collective-permute-done.15 = bf16[6,128,128]{2,1,0:T(8,128)(2,1)S(1)} collective-permute-done((bf16[6,128,128]{2,1,0:T(8,128)(2,1)S(1)}, bf16[6,128,128]{2,1,0:T(8,128)(2,1)S(1)}, u32[]{:S(2)}, u32[]{:S(2)}) %collective-permute-start.15) | collective-permute-done | bytes 196640 | tf_op jit(solution)/shard_map/ppermute | solution.py:417
  266.5 1.9 cayley_pullback.1
  268.4 0.9 copy.11
  269.3 1.6 copy.12
  (53 shorter events, 5.0 us)
Async XLA Ops:
  7.2 123.8 %all-gather.2.cloned.1.call-start = ((), (), s32[]{:S(2)}) async-start(), calls=%async_computation.4 | async-start | bytes 13369344 | tf_op jit(solution)/shard_map/all_gather | solution.py:450
  11.4 11.2 %copy-start.9 = (f32[6,128,128]{2,1,0:T(8,128)S(1)}, f32[6,128,128]{2,1,0:T(8,128)}, u32[]{:S(2)}) copy-start(f32[6,128,128]{2,1,0:T(8,128)} %skew_ref) | copy-start | bytes 1179652
  11.4 53.6 %all-to-all-start = ((bf16[16,3,128,128]{3,2,1,0:T(8,128)(2,1)}), bf16[16,3,128,128]{3,2,1,0:T(8,128)(2,1)S(1)}, u32[]{:S(2)}, u32[]{:S(2)}) async-start(bf16[16,3,128,128]{3,2,1,0:T(8,128)(2,1)} %bitcast.35), calls=%async_computation | async-start | bytes 3145728 | tf_op jit(solution)/shard_map/all_to_all | solution.py:452
  43.8 12.0 %collective-permute-start = (bf16[6,128,128]{2,1,0:T(8,128)(2,1)S(1)}, bf16[6,128,128]{2,1,0:T(8,128)(2,1)S(1)}, u32[]{:S(2)}, u32[]{:S(2)}) collective-permute-start(bf16[6,128,128]{2,1,0:T(8,128)(2,1)S(1)} %get-tuple-element.28), channel_id=1, source_target_pairs={{0,32},{32,64},{64,96},{96,0},{1,33},{33,65},{65,97},{97,1},{2,34}... | collective-permute-start | bytes 589832 | tf_op jit(solution)/shard_map/ppermute | solution.py:402
  44.1 11.7 %collective-permute-start.1 = (bf16[6,128,128]{2,1,0:T(8,128)(2,1)S(1)}, bf16[6,128,128]{2,1,0:T(8,128)(2,1)S(1)}, u32[]{:S(2)}, u32[]{:S(2)}) collective-permute-start(bf16[6,128,128]{2,1,0:T(8,128)(2,1)S(1)} %get-tuple-element.28), channel_id=1, source_target_pairs={{0,96},{32,0},{64,32},{96,64},{1,97},{33,1},{65,33},{97,65},{2,98}... | collective-permute-start | bytes 589832 | tf_op jit(solution)/shard_map/ppermute | solution.py:402
  45.9 19.0 %collective-permute-start.2 = (bf16[6,128,128]{2,1,0:T(8,128)(2,1)S(1)}, bf16[6,128,128]{2,1,0:T(8,128)(2,1)S(1)}, u32[]{:S(2)}, u32[]{:S(2)}) collective-permute-start(bf16[6,128,128]{2,1,0:T(8,128)(2,1)S(1)} %get-tuple-element.28), channel_id=1, source_target_pairs={{0,64},{32,96},{64,0},{96,32},{1,65},{33,97},{65,1},{97,33},{2,66}... | collective-permute-start | bytes 589832 | tf_op jit(solution)/shard_map/ppermute | solution.py:402
  65.0 1.1 copy-start.12
  80.6 33.1 %all-to-all-start.1 = ((bf16[16,128,128]{2,1,0:T(8,128)(2,1)}), bf16[16,128,128]{2,1,0:T(8,128)(2,1)S(1)}, u32[]{:S(2)}, u32[]{:S(2)}) async-start(bf16[16,128,128]{2,1,0:T(8,128)(2,1)} %get-tuple-element.31), calls=%async_computation.1 | async-start | bytes 1048576 | tf_op jit(solution)/shard_map/all_to_all | solution.py:457
  90.1 22.5 %collective-permute-start.3 = (bf16[12,128,128]{2,1,0:T(8,128)(2,1)S(1)}, bf16[12,128,128]{2,1,0:T(8,128)(2,1)S(1)}, u32[]{:S(2)}, u32[]{:S(2)}) collective-permute-start(bf16[12,128,128]{2,1,0:T(8,128)(2,1)S(1)} %get-tuple-element.59), channel_id=1, source_target_pairs={{0,128},{128,8},{8,136},{136,0},{1,129},{129,9},{9,137},{137,1},{2... | collective-permute-start | bytes 1179656 | tf_op jit(solution)/shard_map/ppermute | solution.py:408
  90.2 23.4 %collective-permute-start.4 = (bf16[12,128,128]{2,1,0:T(8,128)(2,1)S(1)}, bf16[12,128,128]{2,1,0:T(8,128)(2,1)S(1)}, u32[]{:S(2)}, u32[]{:S(2)}) collective-permute-start(bf16[12,128,128]{2,1,0:T(8,128)(2,1)S(1)} %get-tuple-element.60), channel_id=1, source_target_pairs={{0,136},{128,0},{8,128},{136,8},{1,137},{129,1},{9,129},{137,9},{2... | collective-permute-start | bytes 1179656 | tf_op jit(solution)/shard_map/ppermute | solution.py:408
  93.5 24.6 %copy-start.10 = (s32[4,96]{1,0:T(4,128)S(1)}, s32[4,96]{1,0:T(4,128)}, u32[]{:S(2)}) copy-start(s32[4,96]{1,0:T(4,128)} %order_ref.3) | copy-start | bytes 4612
  113.7 0.8 copy-start.13
  114.6 3.5 %collective-permute-start.5 = (bf16[48,128,128]{2,1,0:T(8,128)(2,1)S(1)}, bf16[48,128,128]{2,1,0:T(8,128)(2,1)S(1)}, u32[]{:S(2)}, u32[]{:S(2)}) collective-permute-start(bf16[48,128,128]{2,1,0:T(8,128)(2,1)S(1)} %constant_dynamic-update-slice_fusion.near_ref), channel_id=1, source_target_pairs={{0,16},{16,0},{1,17},{17,1},{2,18},{18,2},{3,19},{19,3},{4,20},{20... | collective-permute-start | bytes 4718600 | tf_op jit(solution)/shard_map/ppermute | solution.py:397
  118.1 1.1 copy-start.6
  126.7 1.8 copy-start
  128.5 1.6 copy-start.2
  130.1 0.9 copy-start.8
  131.0 21.8 %copy-start.1 = (bf16[4,3072,128]{2,1,0:T(8,128)(2,1)S(1)}, bf16[4,3072,128]{2,1,0:T(8,128)(2,1)}, u32[]{:S(2)}) copy-start(bf16[4,3072,128]{2,1,0:T(8,128)(2,1)} %copy-done) | copy-start | bytes 9437188
  143.0 27.0 %all-to-all-start.2 = ((bf16[16,128,128]{2,1,0:T(8,128)(2,1)}), bf16[16,128,128]{2,1,0:T(8,128)(2,1)}, u32[]{:S(2)}, u32[]{:S(2)}) async-start(bf16[16,128,128]{2,1,0:T(8,128)(2,1)} %bitcast.38), calls=%async_computation.2 | async-start | bytes 1048576 | tf_op jit(solution)/shard_map/all_to_all | solution.py:461
  152.8 1.9 copy-start.3
  154.7 1.1 copy-start.7
  165.1 1.2 copy-start.4
  166.3 1.2 copy-start.11
  170.0 3.6 %collective-permute-start.6 = (bf16[8,6,128,128]{3,2,1,0:T(8,128)(2,1)}, bf16[8,6,128,128]{3,2,1,0:T(8,128)(2,1)S(1)}, u32[]{:S(2)}, u32[]{:S(2)}) collective-permute-start(bf16[8,6,128,128]{3,2,1,0:T(8,128)(2,1)} %copy-done.11), channel_id=1, source_target_pairs={{0,16},{16,0},{1,17},{17,1},{2,18},{18,2},{3,19},{19,3},{4,20},{20... | collective-permute-start | bytes 4718600 | tf_op jit(solution)/shard_map/ppermute | solution.py:397
  173.6 2.0 copy-start.14
  175.6 17.9 %collective-permute-start.7 = (bf16[2,6,128,128]{3,2,1,0:T(8,128)(2,1)S(1)}, bf16[2,6,128,128]{3,2,1,0:T(8,128)(2,1)S(1)}, u32[]{:S(2)}, u32[]{:S(2)}) collective-permute-start(bf16[2,6,128,128]{3,2,1,0:T(8,128)(2,1)S(1)} %get-tuple-element.57), channel_id=1, source_target_pairs={{0,128},{128,8},{8,136},{136,0},{1,129},{129,9},{9,137},{137,1},{2... | collective-permute-start | bytes 1179656 | tf_op jit(solution)/shard_map/ppermute | solution.py:408
  176.2 17.3 %collective-permute-start.8 = (bf16[2,6,128,128]{3,2,1,0:T(8,128)(2,1)S(1)}, bf16[2,6,128,128]{3,2,1,0:T(8,128)(2,1)S(1)}, u32[]{:S(2)}, u32[]{:S(2)}) collective-permute-start(bf16[2,6,128,128]{3,2,1,0:T(8,128)(2,1)S(1)} %get-tuple-element.58), channel_id=1, source_target_pairs={{0,136},{128,0},{8,128},{136,8},{1,137},{129,1},{9,129},{137,9},{2... | collective-permute-start | bytes 1179656 | tf_op jit(solution)/shard_map/ppermute | solution.py:408
  194.4 6.0 %copy-start.5 = (bf16[8,6,128,128]{3,2,1,0:T(8,128)(2,1)S(1)}, bf16[8,6,128,128]{3,2,1,0:T(8,128)(2,1)}, u32[]{:S(2)}) copy-start(bf16[8,6,128,128]{3,2,1,0:T(8,128)(2,1)} %copy-done.4) | copy-start | bytes 4718596
  194.5 73.9 %all-to-all-start.3 = ((bf16[16,3,128,128]{3,2,1,0:T(8,128)(2,1)}), bf16[16,3,128,128]{3,2,1,0:T(8,128)(2,1)S(1)}, u32[]{:S(2)}, u32[]{:S(2)}) async-start(bf16[16,3,128,128]{3,2,1,0:T(8,128)(2,1)} %attend_back.1), calls=%async_computation.3 | async-start | bytes 3145728 | tf_op jit(solution)/shard_map/all_to_all | solution.py:471
  202.2 7.9 %collective-permute-start.10 = (bf16[6,128,128]{2,1,0:T(8,128)(2,1)S(1)}, bf16[6,128,128]{2,1,0:T(8,128)(2,1)S(1)}, u32[]{:S(2)}, u32[]{:S(2)}) collective-permute-start(bf16[6,128,128]{2,1,0:T(8,128)(2,1)S(1)} %get-tuple-element.56), channel_id=1, source_target_pairs={{0,32},{32,64},{64,96},{96,0},{1,33},{33,65},{65,97},{97,1},{2,34}... | collective-permute-start | bytes 589832 | tf_op jit(solution)/shard_map/ppermute | solution.py:402
  202.8 11.2 %collective-permute-start.11 = (bf16[6,128,128]{2,1,0:T(8,128)(2,1)S(1)}, bf16[6,128,128]{2,1,0:T(8,128)(2,1)S(1)}, u32[]{:S(2)}, u32[]{:S(2)}) collective-permute-start(bf16[6,128,128]{2,1,0:T(8,128)(2,1)S(1)} %get-tuple-element.55), channel_id=1, source_target_pairs={{0,96},{32,0},{64,32},{96,64},{1,97},{33,1},{65,33},{97,65},{2,98}... | collective-permute-start | bytes 589832 | tf_op jit(solution)/shard_map/ppermute | solution.py:402
  204.3 9.7 %collective-permute-start.9 = (bf16[6,128,128]{2,1,0:T(8,128)(2,1)S(1)}, bf16[6,128,128]{2,1,0:T(8,128)(2,1)S(1)}, u32[]{:S(2)}, u32[]{:S(2)}) collective-permute-start(bf16[6,128,128]{2,1,0:T(8,128)(2,1)S(1)} %get-tuple-element.54), channel_id=1, source_target_pairs={{0,64},{32,96},{64,0},{96,32},{1,65},{33,97},{65,1},{97,33},{2,66}... | collective-permute-start | bytes 589832 | tf_op jit(solution)/shard_map/ppermute | solution.py:402
  214.2 9.7 %collective-permute-start.12 = (bf16[6,128,128]{2,1,0:T(8,128)(2,1)S(1)}, bf16[6,128,128]{2,1,0:T(8,128)(2,1)S(1)}, u32[]{:S(2)}, u32[]{:S(2)}) collective-permute-start(bf16[6,128,128]{2,1,0:T(8,128)(2,1)S(1)} %fusion.2), channel_id=1, source_target_pairs={{0,8},{8,0},{1,9},{9,1},{2,10},{10,2},{3,11},{11,3},{4,12},{12,4},... | collective-permute-start | bytes 589832 | tf_op jit(solution)/shard_map/ppermute | solution.py:417
  223.9 16.4 %collective-permute-start.13 = (bf16[6,128,128]{2,1,0:T(8,128)(2,1)S(1)}, bf16[6,128,128]{2,1,0:T(8,128)(2,1)S(1)}, u32[]{:S(2)}, u32[]{:S(2)}) collective-permute-start(bf16[6,128,128]{2,1,0:T(8,128)(2,1)S(1)} %add_convert_fusion.5), channel_id=1, source_target_pairs={{0,1},{1,0},{2,3},{3,2},{4,5},{5,4},{6,7},{7,6},{8,9},{9,8},{10,11... | collective-permute-start | bytes 589832 | tf_op jit(solution)/shard_map/ppermute | solution.py:417
  240.4 10.9 %collective-permute-start.14 = (bf16[6,128,128]{2,1,0:T(8,128)(2,1)S(1)}, bf16[6,128,128]{2,1,0:T(8,128)(2,1)S(1)}, u32[]{:S(2)}, u32[]{:S(2)}) collective-permute-start(bf16[6,128,128]{2,1,0:T(8,128)(2,1)S(1)} %add_convert_fusion.4), channel_id=1, source_target_pairs={{0,2},{1,3},{2,0},{3,1},{4,6},{5,7},{6,4},{7,5},{8,10},{9,11},{10,... | collective-permute-start | bytes 589832 | tf_op jit(solution)/shard_map/ppermute | solution.py:417
  251.3 15.1 %collective-permute-start.15 = (bf16[6,128,128]{2,1,0:T(8,128)(2,1)S(1)}, bf16[6,128,128]{2,1,0:T(8,128)(2,1)S(1)}, u32[]{:S(2)}, u32[]{:S(2)}) collective-permute-start(bf16[6,128,128]{2,1,0:T(8,128)(2,1)S(1)} %add_convert_fusion.3), channel_id=1, source_target_pairs={{0,4},{1,5},{2,6},{3,7},{4,0},{5,1},{6,2},{7,3},{8,12},{9,13},{10,... | collective-permute-start | bytes 589832 | tf_op jit(solution)/shard_map/ppermute | solution.py:417
Sparse Core Ops, SparseCore 0:
  9.8 105.2 all-gather.1

commit v2 on v1

--- a/solution.py
+++ b/solution.py
@@ -19,7 +19,9 @@
 HIGH = lax.Precision.HIGHEST
 ROWS = ("xl", "y", "c")
 SEQ = ("xh", "z")
-QB = 256
+QB = 512
+KB = 2048
+PANEL = 32
 LOG2E = 1.4426950408889634
 MIB = 1024 * 1024
 
@@ -33,41 +35,38 @@
     row = lax.broadcasted_iota(jnp.int32, (size, size), 0)
     col = lax.broadcasted_iota(jnp.int32, (size, size), 1)
     eye = (row == col).astype(F32)
-    row8 = lax.broadcasted_iota(jnp.int32, (8, size), 0)
-    col8 = lax.broadcasted_iota(jnp.int32, (8, size), 1)
-    eye8 = (row8 == col8).astype(F32)
-    rowp = lax.broadcasted_iota(jnp.int32, (size, 8), 0)
-    colp = lax.broadcasted_iota(jnp.int32, (size, 8), 1)
+    eye_panel = eye[:PANEL]
+    rowp = lax.broadcasted_iota(jnp.int32, (size, PANEL), 0)
+    colp = lax.broadcasted_iota(jnp.int32, (size, PANEL), 1)
     for b in range(count):
         params_b = skew_ref[b]
         inv_ref[b] = eye + params_b - params_b.T
 
     def step(g, carry):
-        first = pl.multiple_of(g * 8, 8)
-        panels = [inv_ref[b, pl.ds(first, 8), :] for b in range(count)]
-        sides = [eye8] * count
-        for j in range(8):
-            pick = (lax.broadcasted_iota(jnp.int32, (8, 1), 0) == j).astype(F32)
+        first = pl.multiple_of(g * PANEL, PANEL)
+        panels = [inv_ref[b, pl.ds(first, PANEL), :] for b in range(count)]
+        sides = [eye_panel] * count
+        for j in range(PANEL):
+            pick = (lax.broadcasted_iota(jnp.int32, (PANEL, 1), 0) == j).astype(F32)
             for b in range(count):
                 panel, side = panels[b], sides[b]
-                column = panel[:, j : j + 1]
                 scale = 1.0 / panel[j : j + 1, j : j + 1]
-                left = (column - pick) * scale
-                panels[b] = panel - left * panel[j : j + 1, :]
-                sides[b] = side - left * side[j : j + 1, :]
+                left = panel[:, j : j + 1] - pick
+                panels[b] = panel - left * (panel[j : j + 1, :] * scale)
+                sides[b] = side - left * (side[j : j + 1, :] * scale)
         selector = (rowp - first == colp).astype(F32)
         for b in range(count):
             whole = inv_ref[b]
             update = jnp.dot(
-                whole[:, :8] - selector,
+                whole[:, :PANEL] - selector,
                 panels[b] + sides[b],
                 precision=HIGH,
                 preferred_element_type=F32,
             )
-            inv_ref[b] = pltpu.roll(whole - update, size - 8, 1)
+            inv_ref[b] = pltpu.roll(whole - update, size - PANEL, 1)
         return carry
 
-    lax.fori_loop(0, size // 8, step, 0)
+    lax.fori_loop(0, size // PANEL, step, 0)
     for b in range(count):
         rot_ref[b] = (2.0 * inv_ref[b] - eye).astype(BF)
 
@@ -108,15 +107,25 @@
         vt_ref[...] = v_ref[...].reshape(-1, HD).T
 
     queries = q_ref[...].reshape(QB, HD)
-    keys = k_ref[...].reshape(-1, HD)
-    scores = lax.dot_general(keys, queries, (((1,), (1,)), ((), ())), preferred_element_type=F32)
+    groups, _, tok, _ = k_ref.shape
+    length = groups * tok
+    per = KB // tok
     factor = LOG2E / math.sqrt(HD)
-    top = jnp.max(scores, axis=0, keepdims=True)
-    exps = jnp.exp2((scores - top) * factor)
-    total = jnp.sum(exps, axis=0, keepdims=True)
-    low = exps.astype(BF)
-    exps_ref[0] = low
-    wide = jnp.dot(vt_ref[...], low, preferred_element_type=F32) / total
+    scores = []
+    for c in range(length // KB):
+        keys = k_ref[c * per : (c + 1) * per].reshape(KB, HD)
+        scores.append(
+            lax.dot_general(keys, queries, (((1,), (1,)), ((), ())), preferred_element_type=F32)
+        )
+    top = functools.reduce(jnp.maximum, [jnp.max(s, axis=0, keepdims=True) for s in scores])
+    total, wide = 0.0, 0.0
+    for c, part in enumerate(scores):
+        exps = jnp.exp2((part - top) * factor)
+        total += jnp.sum(exps, axis=0, keepdims=True)
+        low = exps.astype(BF)
+        exps_ref[0, c * KB : (c + 1) * KB, :] = low
+        wide += jnp.dot(vt_ref[:, c * KB : (c + 1) * KB], low, preferred_element_type=F32)
+    wide = wide / total
     wide_ref[0] = wide
     sums_ref[0] = 1.0 / total
     att_ref[...] = wide.T.astype(BF).reshape(att_ref.shape)
@@ -170,19 +179,24 @@
         dv_ref[...] = jnp.zeros_like(dv_ref)
 
     queries = q_ref[...].reshape(QB, HD)
-    values = v_ref[...].reshape(-1, HD)
     dout = jnp.concatenate([dout_ref[p] for p in range(per)], axis=1)
     inv_sum = sums_ref[0]
     wide_dout = dout.astype(F32)
-    low = exps_ref[0]
-    dv_ref[...] += lax.dot_general(
-        low, (wide_dout * inv_sum).astype(BF), (((1,), (1,)), ((), ())), preferred_element_type=F32
-    )
+    dout_low = (wide_dout * inv_sum).astype(BF)
     centre = jnp.sum(wide_dout * wide_ref[0], axis=0, keepdims=True)
-    dprobs = jnp.dot(values, dout, preferred_element_type=F32)
-    dscores = (low.astype(F32) * ((dprobs - centre) * (inv_sum * (1.0 / math.sqrt(HD))))).astype(BF)
-    dk_ref[...] += jnp.dot(dscores, queries, preferred_element_type=F32)
-    dq = jnp.dot(kt_ref[...], dscores, preferred_element_type=F32)
+    factor = inv_sum * (1.0 / math.sqrt(HD))
+    dq = 0.0
+    for c in range(groups * tok // KB):
+        at = slice(c * KB, (c + 1) * KB)
+        values = v_ref[c * KB // tok : (c + 1) * KB // tok].reshape(KB, HD)
+        low = exps_ref[0, at, :]
+        dprobs = jnp.dot(values, dout, preferred_element_type=F32)
+        dscores = (low.astype(F32) * ((dprobs - centre) * factor)).astype(BF)
+        dv_ref[at, :] += lax.dot_general(
+            low, dout_low, (((1,), (1,)), ((), ())), preferred_element_type=F32
+        )
+        dk_ref[at, :] += jnp.dot(dscores, queries, preferred_element_type=F32)
+        dq += jnp.dot(kt_ref[:, at], dscores, preferred_element_type=F32)
     out_ref[pl.ds(step * per, per), 0] = dq.T.astype(BF).reshape(per, tok, HD)
 
     @pl.when(step == pl.num_programs(0) - 1)
@@ -296,52 +310,83 @@
 
 
 def up_kernel(order_ref, self_ref, proj_ref, flip_ref, moved_ref, out_ref, mine_ref, other_ref, a_ref, b_ref):
-    blocks = proj_ref.shape[1] // BS
+    step = pl.program_id(0)
+    width = proj_ref.shape[1]
+    blocks = width // BS
     owned = mine_ref.shape[1]
-    xl, y, core = self_ref[0], self_ref[1], self_ref[2]
-    for j in range(blocks):
-        a_ref[j * BS : (j + 1) * BS, :] = proj_ref[:, j * BS : (j + 1) * BS].T
-    source, target = a_ref, b_ref
-    for factor in range(FACTORS):
+    core = self_ref[2]
+    factor, pair = step // 2, step % 2
+
+    @pl.when(step == 0)
+    def _():
+        for j in range(blocks):
+            a_ref[j * BS : (j + 1) * BS, :] = proj_ref[:, j * BS : (j + 1) * BS].T
+
+    def turn_over(source, target):
         for half, grad_ref in ((core, mine_ref), (1 - core, other_ref)):
-
-            def body(i, carry, factor=factor, source=source, target=target, half=half, grad_ref=grad_ref):
-                pair, inside = i // owned, i % owned
-                j = (2 * pair + half) * owned + inside
-                at = factor * blocks + j
-                block = gather_block(order_ref, factor, j, source)
-                mixed = jnp.dot(flip_ref[at], block, preferred_element_type=F32).astype(BF)
-                scatter_block(order_ref, factor, j, mixed, target)
-                moved = moved_ref[factor, pl.ds(pl.multiple_of(j * BS, BS), BS), :]
-                owner = factor * (blocks // (2 * owned)) + pair
-                slot = ((owner // 4) ^ xl) * 4 + ((owner % 4 + 4 - y) % 4)
-                grad_ref[slot, inside] = lax.dot_general(
+            for i in range(owned):
+                inside = half * owned + i
+                places = [
+                    pl.multiple_of(
+                        order_ref[factor, (2 * owned * pair + inside) * PER + p] * PIECE, PIECE
+                    )
+                    for p in range(PER)
+                ]
+                block = jnp.concatenate([source[pl.ds(at, PIECE), :] for at in places], axis=0)
+                mixed = jnp.dot(flip_ref[inside], block, preferred_element_type=F32).astype(BF)
+                for p, at in enumerate(places):
+                    target[pl.ds(at, PIECE), :] = mixed[p * PIECE : (p + 1) * PIECE, :]
+                moved = moved_ref[0, pl.ds(pl.multiple_of(inside * BS, BS), BS), :]
+                grad_ref[0, i] = lax.dot_general(
                     block, moved, (((1,), (1,)), ((), ())), preferred_element_type=F32
                 ).astype(BF)
-                return carry
-
-            lax.fori_loop(0, blocks // 2, body, 0, unroll=4)
-        source, target = target, source
-    for j in range(blocks):
-        out_ref[:, j * BS : (j + 1) * BS] = source[j * BS : (j + 1) * BS, :].T
+
+    @pl.when(factor % 2 == 0)
+    def _():
+        turn_over(a_ref, b_ref)
+
+    @pl.when(factor % 2 == 1)
+    def _():
+        turn_over(b_ref, a_ref)
+
+    @pl.when(step == pl.num_programs(0) - 1)
+    def _():
+        for j in range(blocks):
+            out_ref[:, j * BS : (j + 1) * BS] = a_ref[j * BS : (j + 1) * BS, :].T
 
 
 def up(orders, position, projected, flipped, moved):
     tok, width = projected.shape
-    smem = pl.BlockSpec(memory_space=pltpu.SMEM)
-    vmem = pl.BlockSpec(memory_space=pltpu.VMEM)
     owned = flipped.shape[0] // 16
-    half = jax.ShapeDtypeStruct((8, owned, BS, BS), BF)
+    pairs = 8
+    rows = FACTORS * width // pairs
+    half = jax.ShapeDtypeStruct((pairs, owned, BS, BS), BF)
+
+    def slot(t, order_ref, self_ref):
+        return ((t // 4) ^ self_ref[0]) * 4 + (t % 4 + 4 - self_ref[1]) % 4, 0, 0, 0
+
     return pl.pallas_call(
         up_kernel,
-        in_specs=[smem, smem, vmem, vmem, vmem],
-        out_specs=[vmem, vmem, vmem],
+        grid_spec=pltpu.PrefetchScalarGridSpec(
+            num_scalar_prefetch=2,
+            grid=(pairs,),
+            in_specs=[
+                pl.BlockSpec((tok, width), lambda t, *_: (0, 0)),
+                pl.BlockSpec((2 * owned, BS, BS), lambda t, *_: (t, 0, 0)),
+                pl.BlockSpec((1, rows, tok), lambda t, *_: (t, 0, 0)),
+            ],
+            out_specs=[
+                pl.BlockSpec((tok, width), lambda t, *_: (0, 0)),
+                pl.BlockSpec((1, owned, BS, BS), slot),
+                pl.BlockSpec((1, owned, BS, BS), slot),
+            ],
+            scratch_shapes=[pltpu.VMEM((width, tok), BF), pltpu.VMEM((width, tok), BF)],
+        ),
         out_shape=[jax.ShapeDtypeStruct((tok, width), BF), half, half],
-        scratch_shapes=[pltpu.VMEM((width, tok), BF), pltpu.VMEM((width, tok), BF)],
-        compiler_params=params(40),
+        compiler_params=params(58, ("arbitrary",)),
         cost_estimate=pl.CostEstimate(flops=10**9, bytes_accessed=10**7, transcendentals=0),
         name="butterfly_up",
-    )(orders, position, projected, flipped, moved)
+    )(orders, position, projected, flipped, moved.reshape(pairs, rows, tok))
 
 
 def products_kernel(weight_ref, up_ref, att_ref, back_ref, proj_ref, acc_ref):
@@ -367,7 +412,7 @@
 def products(weight, upstream, att):
     rows, width = weight.shape
     tok = upstream.shape[1]
-    tile = 256
+    tile = 512
     return pl.pallas_call(
         products_kernel,
         grid=(rows // tile,),
@@ -429,9 +474,9 @@
     return jnp.concatenate([own, shift(own, "y", 1), shift(own, "y", 3), shift(own, "y", 2)], axis=0)
 
 
-def gather_blocks(column, earlier):
+def gather_blocks(column, crossed):
     count = column.shape[0] // 4
-    near = jnp.concatenate([column, after(cross(column), earlier)], axis=0)
+    near = jnp.concatenate([column, crossed], axis=0)
     far = swap(near, "c")
     at = jnp.arange(16 * count, dtype=jnp.int32)
     slot, inside = at // count, at % count
@@ -452,11 +497,12 @@
     spread = lax.all_to_all(rows, SEQ, split_axis=0, concat_axis=0, tiled=True)
     inverse, rot_own = cayley(after(skew_params, rows))
     column = gather_column(rot_own)
-    spread, column = lax.optimization_barrier((spread, column))
+    crossed = cross(column)
+    spread, crossed = lax.optimization_barrier((spread, crossed))
     att, wide, exps, sums = attend(spread)
     att_own = lax.all_to_all(att, SEQ, split_axis=0, concat_axis=0, tiled=True)
-    near, far, home = gather_blocks(column, att_own)
-    moved_grad, upstream, flipped = down(piece_orders, home, cotangent[0], near, far)
+    near, far, home = gather_blocks(column, crossed)
+    moved_grad, upstream, flipped = down(piece_orders, home, cotangent[0], near, after(far, att))
     grad_att, projected = products(weight, upstream, att_own)
     dout = lax.all_to_all(
         grad_att.reshape(seqs, HD, tok), SEQ, split_axis=0, concat_axis=0, tiled=True
@@ -464,16 +510,21 @@
     block_output, mine, other = up(piece_orders, position, projected, flipped, moved_grad)
     mine, other, dout = lax.optimization_barrier((mine, other, dout))
     from_core = swap(other, "c")
-    send = add(mine[4:], from_core[4:])
-    from_xl = cross(send)
-    grads = attend_back(spread, after(dout, send), wide, exps, sums)
-    from_xl, grads = lax.optimization_barrier((from_xl, grads))
+    grads = attend_back(spread, dout, wide, exps, sums)
+    from_core, grads = lax.optimization_barrier((from_core, grads))
     grads = lax.all_to_all(grads, SEQ, split_axis=0, concat_axis=0, tiled=True)
     grad_inputs = grads.transpose(2, 1, 0, 3).reshape(1, tok, 3, seqs * HD)
+    from_xl = cross(add(mine[4:], from_core[4:]))
     share = add(mine[:4], from_core[:4], from_xl)
-    owner_grad = add(share[0], *[shift(share[dy], "y", dy) for dy in (2, 1, 3)])
-    for axis, bit in (("xh", 1), ("z", 1), ("z", 2), ("z", 4)):
-        owner_grad = add(owner_grad, partner(owner_grad, axis, bit))
+    share = add(share[0], *[shift(share[dy], "y", dy) for dy in (2, 1, 3)])
+    share = add(share, partner(share, "xh", 1))
+    shape = share.shape
+    parts = lax.all_to_all(
+        after(share, grads).reshape(8, -1, BS), "z", split_axis=0, concat_axis=0, tiled=True
+    )
+    part = add(*[parts[i] for i in range(8)])
+    copies = jnp.broadcast_to(part[None], parts.shape)
+    owner_grad = lax.all_to_all(copies, "z", split_axis=0, concat_axis=0, tiled=True).reshape(shape)
     total_tokens = 16 * tok * seqs
     grad_skew = cayley_pullback(inverse, owner_grad, 1.0 / math.sqrt(total_tokens))
     return block_output[None], grad_inputs, grad_skew

time: 279 us -> 253 us (0.907)
  blocking collectives: 0 us -> 16.8 us
  starting transfers between devices: 63.5 us -> 48.6 us
  Pallas kernels: 80.8 us -> 67.5 us
  waiting for transfers between devices: 94.9 us -> 82.4 us
    ppermute x4 -> x1, waiting for transfers between devices: 37.1 us -> 7.1 us  [partner(): lax.ppermute(x, axis, [(i, i ^ bit) for i in range(lax.axis_size(axis))])]
    all_to_all x0 -> x1, blocking collectives: none -> 16.8 us  [local(): lax.all_to_all(after(share, grads).reshape(8, -1, BS), 'z', split_axis=0,...]
    ppermute x4 -> x1, starting transfers between devices: 15 us -> 0.16 us  [partner(): lax.ppermute(x, axis, [(i, i ^ bit) for i in range(lax.axis_size(axis))])]
    ppermute x4, waiting for transfers between devices: 20.1 us -> 32.4 us  [turn(): lax.ppermute(x, ('xl', 'xh'), [(at[i], at[(i + by) % 4]) for i in range(4)])]
    pallas_call x1, Pallas kernels: 21.2 us -> 14 us  [cayley(): pl.pallas_call(inverse_kernel, out_shape=(jax.ShapeDtypeStruct(skew.shape...]
    ppermute x2, waiting for transfers between devices: 6.97 us -> 0.01 us  [swap(): return lax.ppermute(x, axis, [(0, 1), (1, 0)])]
    all_to_all x0 -> x1, waiting for transfers between devices: none -> 5.53 us  [local(): lax.all_to_all(copies, 'z', split_axis=0, concat_axis=0, tiled=True)]
    all_to_all x1, waiting for transfers between devices: 0.01 us -> 4.59 us  [local(): att_own = lax.all_to_all(att, SEQ, split_axis=0, concat_axis=0, tiled=True)]
  transfers between devices with their start and end apart: 21 -> 19, of which waited for: 13 -> 11; matrix products, arithmetic and copies ran while one was open for 2% -> 5% of each run, Pallas kernels for 25% -> 22%
where the time goes in v2:
time: 253 us; the launch traced here: 251 us
  waiting for transfers between devices  82.4 us (33%)
  Pallas kernels  67.5 us (27%)
  starting transfers between devices  48.6 us (19%)
  local copies, waits for them, and re-layouts  17.2 us (7%)
  blocking collectives  16.8 us (7%)
  between operations  14.3 us (6%)
  other arithmetic  4.7 us (2%)
    ppermute x4, waiting for transfers between devices, turn(): lax.ppermute(x, ('xl', 'xh'), [(at[i], at[(i + by) % 4]) for i in range(4)])  32.4 us
    ppermute x6, waiting for transfers between devices, shift(): return lax.ppermute(x, axis, [(i, (i + by) % n) for i in range(n)])  25.9 us
    all_to_all x1, blocking collectives, local(): lax.all_to_all(after(share, grads).reshape(8, -1, BS), 'z', split_axis=0,...  16.8 us
    pallas_call x1, Pallas kernels, cayley(): pl.pallas_call(inverse_kernel, out_shape=(jax.ShapeDtypeStruct(skew.shape...  14 us
    pallas_call x1, Pallas kernels, attend_back(): pl.pallas_call(attend_back_kernel, grid=(steps,), in_specs=[pl.BlockSpec(...  12.4 us
    unnamed x24, local copies, waits for them, and re-layouts  12 us
    pallas_call x1, Pallas kernels, attend(): pl.pallas_call(attend_kernel, grid=(steps,), in_specs=[pl.BlockSpec((per,...  11.3 us
    all_to_all x1, starting transfers between devices, local(): spread = lax.all_to_all(rows, SEQ, split_axis=0, concat_axis=0, tiled=True)  11.2 us
  transfers between devices with their start and end apart: 19, of which 11 were waited for; matrix products, arithmetic and copies ran while one was open for 5% of the time, Pallas kernels for 22%

profile of v2, /device:TPU:24, one launch (start us, length us, event | category | flops | bytes accessed | tf_op | source)
XLA Modules:
  0.0 251.4 jit_solution(16708366268744541783)
XLA Ops:
  7.2 0.7 all-gather.2.cloned.1.call-update
  7.9 1.9 copy.9
  9.8 1.6 copy.10
  11.4 11.2 %all-to-all-start = ((bf16[16,3,128,128]{3,2,1,0:T(8,128)(2,1)}), bf16[16,3,128,128]{3,2,1,0:T(8,128)(2,1)S(1)}, u32[]{:S(2)}, u32[]{:S(2)}) async-start(bf16[16,3,128,128]{3,2,1,0:T(8,128)(2,1)} %bitcast.42), calls=%async_computation | async-start | bytes 3145728 | tf_op jit(solution)/shard_map/all_to_all | solution.py:497
  22.6 14.0 %cayley.1 = (f32[6,128,128]{2,1,0:T(8,128)S(1)}, bf16[6,128,128]{2,1,0:T(8,128)(2,1)S(1)}) custom-call(f32[6,128,128]{2,1,0:T(8,128)S(1)} %copy-done.4), custom_call_target="tpu_custom_call" | custom-call | tf_op jit(solution)/shard_map/cayley/pallas_call | solution.py:75
  36.6 0.8 collective-permute-start.1
  37.4 0.9 collective-permute-start.2
  38.3 2.2 collective-permute-start
  40.5 6.1 %collective-permute-done.1 = bf16[6,128,128]{2,1,0:T(8,128)(2,1)S(1)} collective-permute-done((bf16[6,128,128]{2,1,0:T(8,128)(2,1)S(1)}, bf16[6,128,128]{2,1,0:T(8,128)(2,1)S(1)}, u32[]{:S(2)}, u32[]{:S(2)}) %collective-permute-start.1) | collective-permute-done | bytes 196640 | tf_op jit(solution)/shard_map/ppermute | solution.py:447
  46.7 9.6 %collective-permute-done.2 = bf16[6,128,128]{2,1,0:T(8,128)(2,1)S(1)} collective-permute-done((bf16[6,128,128]{2,1,0:T(8,128)(2,1)S(1)}, bf16[6,128,128]{2,1,0:T(8,128)(2,1)S(1)}, u32[]{:S(2)}, u32[]{:S(2)}) %collective-permute-start.2) | collective-permute-done | bytes 196640 | tf_op jit(solution)/shard_map/ppermute | solution.py:447
  56.3 3.1 %collective-permute-start.4 = (bf16[12,128,128]{2,1,0:T(8,128)(2,1)S(1)}, bf16[12,128,128]{2,1,0:T(8,128)(2,1)S(1)}, u32[]{:S(2)}, u32[]{:S(2)}) collective-permute-start(bf16[12,128,128]{2,1,0:T(8,128)(2,1)S(1)} %pad_maximum_fusion.2), channel_id=1, source_target_pairs={{0,136},{128,0},{8,128},{136,8},{1,137},{129,1},{9,129},{137,9},{2... | collective-permute-start | bytes 1179656 | tf_op jit(solution)/shard_map/ppermute | solution.py:453
  59.7 16.6 %collective-permute-done.4 = bf16[12,128,128]{2,1,0:T(8,128)(2,1)S(1)} collective-permute-done((bf16[12,128,128]{2,1,0:T(8,128)(2,1)S(1)}, bf16[12,128,128]{2,1,0:T(8,128)(2,1)S(1)}, u32[]{:S(2)}, u32[]{:S(2)}) %collective-permute-start.4) | collective-permute-done | bytes 393248 | tf_op jit(solution)/shard_map/ppermute | solution.py:453
  76.7 0.9 pad_maximum_fusion
  77.6 1.1 copy-done.6
  78.8 1.3 constant_dynamic-update-slice_fusion.near_ref
  80.1 11.3 %attend.1 = (bf16[16,128,128]{2,1,0:T(8,128)(2,1)}, f32[4,128,512]{2,1,0:T(8,128)}, bf16[4,2048,512]{2,1,0:T(8,128)(2,1)}, f32[4,1,512]{2,1,0:T(1,128)}) custom-call(bf16[16,3,128,128]{3,2,1,0:T(8,128)(2,1)} %copy-done.6, bf16[16,3,128,128]{3,2,1,0:T(8,128)(2,1)} %copy-done.6, bf16[16,3,128,128]{3,2,1,0:T(8,128)(2,1)} %copy-done.6), custom_call_target="tpu_custom_call" | custom-call | flops 2147483648 | bytes 8388608 | tf_op jit(solution)/shard_map/attend/pallas_call | solution.py:139
  91.4 9.8 %all-to-all-start.1 = ((bf16[16,128,128]{2,1,0:T(8,128)(2,1)}), bf16[16,128,128]{2,1,0:T(8,128)(2,1)}, u32[]{:S(2)}, u32[]{:S(2)}) async-start(bf16[16,128,128]{2,1,0:T(8,128)(2,1)} %get-tuple-element.31), calls=%async_computation.1 | async-start | bytes 1048576 | tf_op jit(solution)/shard_map/all_to_all | solution.py:503
  101.3 1.1 copy-done.2
  102.4 7.5 %butterfly_down.1 = (bf16[4,3072,128]{2,1,0:T(8,128)(2,1)S(1)}, bf16[3072,128]{1,0:T(8,128)(2,1)S(1)}, bf16[96,128,128]{2,1,0:T(8,128)(2,1)S(1)}) custom-call(s32[4,96]{1,0:T(4,128)S(1)} %copy-done.5, s32[96]{0:T(128)S(1)} %fusion.4.home_ref, bf16[128,3072]{1,0:T(8,128)(2,1)S(1)} %bitcast.40, ...), custom_call_target="tpu_custom_call" | custom-call | flops 1000000000 | bytes 10000000 | tf_op jit(solution)/shard_map/butterfly_down/pallas_call | solution.py:292
  109.9 1.8 copy-done
  111.7 1.6 copy-done.1
  113.3 0.9 copy-done.3
  114.2 4.6 %all-to-all-done.1.att_ref = bf16[16,128,128]{2,1,0:T(8,128)(2,1)} async-done(((bf16[16,128,128]{2,1,0:T(8,128)(2,1)}), bf16[16,128,128]{2,1,0:T(8,128)(2,1)}, u32[]{:S(2)}, u32[]{:S(2)}) %all-to-all-start.1) | async-done | bytes 524320 | tf_op jit(solution)/shard_map/all_to_all | solution.py:503
  118.8 9.8 %products.1 = (bf16[2048,128]{1,0:T(8,128)(2,1)}, bf16[128,3072]{1,0:T(8,128)(2,1)}) custom-call(bf16[2048,3072]{1,0:T(8,128)(2,1)} %all-gather.2.cloned.1.call-done.weight_ref, bf16[3072,128]{1,0:T(8,128)(2,1)} %copy-done.3, bf16[16,128,128]{2,1,0:T(8,128)(2,1)} %all-to-all-done.1.att_ref), custom_call_target="tpu_custom_call" | custom-call | flops 3221225472 | bytes 12582912 | tf_op jit(solution)/shard_map/products/pallas_call | solution.py:416
  128.6 5.8 %all-to-all-start.2 = ((bf16[16,128,128]{2,1,0:T(8,128)(2,1)}), bf16[16,128,128]{2,1,0:T(8,128)(2,1)S(1)}, u32[]{:S(2)}, u32[]{:S(2)}) async-start(bf16[16,128,128]{2,1,0:T(8,128)(2,1)} %bitcast.46), calls=%async_computation.2 | async-start | bytes 1048576 | tf_op jit(solution)/shard_map/all_to_all | solution.py:507
  134.4 0.6 pad_add_fusion.self_ref
  135.0 10.6 %butterfly_up.1 = (bf16[128,3072]{1,0:T(8,128)(2,1)}, bf16[8,6,128,128]{3,2,1,0:T(8,128)(2,1)}, bf16[8,6,128,128]{3,2,1,0:T(8,128)(2,1)}) custom-call(s32[4,96]{1,0:T(4,128)} %order_ref.3, s32[3]{0:T(128)} %pad_add_fusion.self_ref, bf16[128,3072]{1,0:T(8,128)(2,1)} %get-tuple-element.34.proj_ref, bf16[96,128,128]{2,1,0:T(8,128)(2,1)} %copy-done.1, ...), custom_call_target="tpu_custom_call" | custom-call | flops 1000000000 | bytes 10000000 | tf_op jit(solution)/shard_map/butterfly_up/pallas_call | solution.py:368
  145.6 6.2 %all-to-all-done.2.dout_ref = bf16[16,128,128]{2,1,0:T(8,128)(2,1)S(1)} async-done(((bf16[16,128,128]{2,1,0:T(8,128)(2,1)}), bf16[16,128,128]{2,1,0:T(8,128)(2,1)S(1)}, u32[]{:S(2)}, u32[]{:S(2)}) %all-to-all-start.2) | async-done | bytes 524320 | tf_op jit(solution)/shard_map/all_to_all | solution.py:507
  151.8 0.8 copy-done.7
  152.6 12.4 %attend_back.1 = bf16[16,3,128,128]{3,2,1,0:T(8,128)(2,1)} custom-call(bf16[16,3,128,128]{3,2,1,0:T(8,128)(2,1)} %copy-done.6, bf16[16,3,128,128]{3,2,1,0:T(8,128)(2,1)} %copy-done.6, bf16[16,3,128,128]{3,2,1,0:T(8,128)(2,1)} %copy-done.6, bf16[16,128,128]{2,1,0:T(8,128)(2,1)} %copy-done.7, f32[4,128,512]{2,1,0:T(8,128)} %get-tuple-element.43.wide_ref, ...), custom_call_target="tpu_custom_call" | custom-call | flops 4294967296 | bytes 8388608 | tf_op jit(solution)/shard_map/attend_back/pallas_call | solution.py:213
  165.0 5.0 %all-to-all-start.3 = ((bf16[16,3,128,128]{3,2,1,0:T(8,128)(2,1)}), bf16[16,3,128,128]{3,2,1,0:T(8,128)(2,1)S(1)}, u32[]{:S(2)}, u32[]{:S(2)}) async-start(bf16[16,3,128,128]{3,2,1,0:T(8,128)(2,1)} %attend_back.1), calls=%async_computation.3 | async-start | bytes 3145728 | tf_op jit(solution)/shard_map/all_to_all | solution.py:515
  170.0 1.4 add_convert_fusion.1
  171.4 0.9 collective-permute-start.7
  172.3 2.7 %collective-permute-start.8 = (bf16[2,6,128,128]{3,2,1,0:T(8,128)(2,1)S(1)}, bf16[2,6,128,128]{3,2,1,0:T(8,128)(2,1)S(1)}, u32[]{:S(2)}, u32[]{:S(2)}) collective-permute-start(bf16[2,6,128,128]{3,2,1,0:T(8,128)(2,1)S(1)} %get-tuple-element.58), channel_id=1, source_target_pairs={{0,136},{128,0},{8,128},{136,8},{1,137},{129,1},{9,129},{137,9},{2... | collective-permute-start | bytes 1179656 | tf_op jit(solution)/shard_map/ppermute | solution.py:453
  175.0 15.4 %collective-permute-done.7 = bf16[2,6,128,128]{3,2,1,0:T(8,128)(2,1)S(1)} collective-permute-done((bf16[2,6,128,128]{3,2,1,0:T(8,128)(2,1)S(1)}, bf16[2,6,128,128]{3,2,1,0:T(8,128)(2,1)S(1)}, u32[]{:S(2)}, u32[]{:S(2)}) %collective-permute-start.7) | collective-permute-done | bytes 393248 | tf_op jit(solution)/shard_map/ppermute | solution.py:453
  190.4 1.5 add_convert_fusion
  192.0 0.9 collective-permute-start.10
  192.9 1.2 collective-permute-start.11
  194.4 5.4 %collective-permute-done.10 = bf16[6,128,128]{2,1,0:T(8,128)(2,1)S(1)} collective-permute-done((bf16[6,128,128]{2,1,0:T(8,128)(2,1)S(1)}, bf16[6,128,128]{2,1,0:T(8,128)(2,1)S(1)}, u32[]{:S(2)}, u32[]{:S(2)}) %collective-permute-start.10) | collective-permute-done | bytes 196640 | tf_op jit(solution)/shard_map/ppermute | solution.py:447
  199.9 4.8 %collective-permute-done.11 = bf16[6,128,128]{2,1,0:T(8,128)(2,1)S(1)} collective-permute-done((bf16[6,128,128]{2,1,0:T(8,128)(2,1)S(1)}, bf16[6,128,128]{2,1,0:T(8,128)(2,1)S(1)}, u32[]{:S(2)}, u32[]{:S(2)}) %collective-permute-start.11) | collective-permute-done | bytes 196640 | tf_op jit(solution)/shard_map/ppermute | solution.py:447
  204.9 7.1 %collective-permute-done.12 = bf16[6,128,128]{2,1,0:T(8,128)(2,1)S(1)} collective-permute-done((bf16[6,128,128]{2,1,0:T(8,128)(2,1)S(1)}, bf16[6,128,128]{2,1,0:T(8,128)(2,1)S(1)}, u32[]{:S(2)}, u32[]{:S(2)}) %collective-permute-start.12) | collective-permute-done | bytes 196640 | tf_op jit(solution)/shard_map/ppermute | solution.py:462
  212.1 16.8 %all_to_all.30 = bf16[8,96,128]{2,1,0:T(8,128)(2,1)S(1)} all-to-all(bf16[8,96,128]{2,1,0:T(8,128)(2,1)S(1)} %bitcast.45), channel_id=1, replica_groups=mesh['xl'=2,'y'=4,'c'=2,'xh'=2,'z'=8] {'z'}, dimensions={0} | all-to-all | bytes 393216 | tf_op jit(solution)/shard_map/all_to_all | solution.py:522
  228.9 0.7 broadcast_in_dim.14
  229.6 3.4 %all-to-all-start.5 = ((bf16[8,96,128]{2,1,0:T(8,128)(2,1)}), bf16[8,96,128]{2,1,0:T(8,128)(2,1)S(1)}, u32[]{:S(2)}, u32[]{:S(2)}) async-start(bf16[8,96,128]{2,1,0:T(8,128)(2,1)} %broadcast_in_dim.14), calls=%async_computation.5 | async-start | bytes 393216 | tf_op jit(solution)/shard_map/all_to_all | solution.py:527
  233.0 1.6 copy.11
  234.6 2.6 %copy.12 = bf16[1,128,3,2048]{3,1,2,0:T(8,128)(2,1)} copy(bf16[1,128,3,2048]{1,3,2,0:T(8,128)(2,1)} %bitcast.43) | data formatting | bytes 3145728
  237.2 5.5 %all-to-all-done.5 = bf16[8,96,128]{2,1,0:T(8,128)(2,1)S(1)} async-done(((bf16[8,96,128]{2,1,0:T(8,128)(2,1)}), bf16[8,96,128]{2,1,0:T(8,128)(2,1)S(1)}, u32[]{:S(2)}, u32[]{:S(2)}) %all-to-all-start.5) | async-done | bytes 196640 | tf_op jit(solution)/shard_map/all_to_all | solution.py:527
  242.7 1.9 cayley_pullback.1
  (39 shorter events, 1.6 us)
Async XLA Ops:
  7.2 111.6 %all-gather.2.cloned.1.call-start = ((), (), s32[]{:S(2)}) async-start(), calls=%async_computation.6 | async-start | bytes 13369344 | tf_op jit(solution)/shard_map/all_gather | solution.py:495
  11.4 11.2 %copy-start.4 = (f32[6,128,128]{2,1,0:T(8,128)S(1)}, f32[6,128,128]{2,1,0:T(8,128)}, u32[]{:S(2)}) copy-start(f32[6,128,128]{2,1,0:T(8,128)} %skew_ref) | copy-start | bytes 1179652
  11.4 66.2 %all-to-all-start = ((bf16[16,3,128,128]{3,2,1,0:T(8,128)(2,1)}), bf16[16,3,128,128]{3,2,1,0:T(8,128)(2,1)S(1)}, u32[]{:S(2)}, u32[]{:S(2)}) async-start(bf16[16,3,128,128]{3,2,1,0:T(8,128)(2,1)} %bitcast.42), calls=%async_computation | async-start | bytes 3145728 | tf_op jit(solution)/shard_map/all_to_all | solution.py:497
  36.6 10.1 %collective-permute-start.1 = (bf16[6,128,128]{2,1,0:T(8,128)(2,1)S(1)}, bf16[6,128,128]{2,1,0:T(8,128)(2,1)S(1)}, u32[]{:S(2)}, u32[]{:S(2)}) collective-permute-start(bf16[6,128,128]{2,1,0:T(8,128)(2,1)S(1)} %get-tuple-element.28), channel_id=1, source_target_pairs={{0,96},{32,0},{64,32},{96,64},{1,97},{33,1},{65,33},{97,65},{2,98}... | collective-permute-start | bytes 589832 | tf_op jit(solution)/shard_map/ppermute | solution.py:447
  37.4 18.8 %collective-permute-start.2 = (bf16[6,128,128]{2,1,0:T(8,128)(2,1)S(1)}, bf16[6,128,128]{2,1,0:T(8,128)(2,1)S(1)}, u32[]{:S(2)}, u32[]{:S(2)}) collective-permute-start(bf16[6,128,128]{2,1,0:T(8,128)(2,1)S(1)} %get-tuple-element.28), channel_id=1, source_target_pairs={{0,64},{32,96},{64,0},{96,32},{1,65},{33,97},{65,1},{97,33},{2,66}... | collective-permute-start | bytes 589832 | tf_op jit(solution)/shard_map/ppermute | solution.py:447
  38.3 21.1 %collective-permute-start = (bf16[6,128,128]{2,1,0:T(8,128)(2,1)S(1)}, bf16[6,128,128]{2,1,0:T(8,128)(2,1)S(1)}, u32[]{:S(2)}, u32[]{:S(2)}) collective-permute-start(bf16[6,128,128]{2,1,0:T(8,128)(2,1)S(1)} %get-tuple-element.28), channel_id=1, source_target_pairs={{0,32},{32,64},{64,96},{96,0},{1,33},{33,65},{65,97},{97,1},{2,34}... | collective-permute-start | bytes 589832 | tf_op jit(solution)/shard_map/ppermute | solution.py:447
  56.3 20.0 %collective-permute-start.4 = (bf16[12,128,128]{2,1,0:T(8,128)(2,1)S(1)}, bf16[12,128,128]{2,1,0:T(8,128)(2,1)S(1)}, u32[]{:S(2)}, u32[]{:S(2)}) collective-permute-start(bf16[12,128,128]{2,1,0:T(8,128)(2,1)S(1)} %pad_maximum_fusion.2), channel_id=1, source_target_pairs={{0,136},{128,0},{8,128},{136,8},{1,137},{129,1},{9,129},{137,9},{2... | collective-permute-start | bytes 1179656 | tf_op jit(solution)/shard_map/ppermute | solution.py:453
  59.5 17.2 %collective-permute-start.3 = (bf16[12,128,128]{2,1,0:T(8,128)(2,1)S(1)}, bf16[12,128,128]{2,1,0:T(8,128)(2,1)S(1)}, u32[]{:S(2)}, u32[]{:S(2)}) collective-permute-start(bf16[12,128,128]{2,1,0:T(8,128)(2,1)S(1)} %pad_maximum_fusion.1), channel_id=1, source_target_pairs={{0,128},{128,8},{8,136},{136,0},{1,129},{129,9},{9,137},{137,1},{2... | collective-permute-start | bytes 1179656 | tf_op jit(solution)/shard_map/ppermute | solution.py:453
  77.6 1.1 copy-start.6
  80.0 21.2 %copy-start.5 = (s32[4,96]{1,0:T(4,128)S(1)}, s32[4,96]{1,0:T(4,128)}, u32[]{:S(2)}) copy-start(s32[4,96]{1,0:T(4,128)} %order_ref.3) | copy-start | bytes 4612
  80.0 21.2 %collective-permute-start.5 = (bf16[48,128,128]{2,1,0:T(8,128)(2,1)S(1)}, bf16[48,128,128]{2,1,0:T(8,128)(2,1)S(1)}, u32[]{:S(2)}, u32[]{:S(2)}) collective-permute-start(bf16[48,128,128]{2,1,0:T(8,128)(2,1)S(1)} %constant_dynamic-update-slice_fusion.near_ref), channel_id=1, source_target_pairs={{0,16},{16,0},{1,17},{17,1},{2,18},{18,2},{3,19},{19,3},{4,20},{20... | collective-permute-start | bytes 4718600 | tf_op jit(solution)/shard_map/ppermute | solution.py:442
  91.4 27.4 %all-to-all-start.1 = ((bf16[16,128,128]{2,1,0:T(8,128)(2,1)}), bf16[16,128,128]{2,1,0:T(8,128)(2,1)}, u32[]{:S(2)}, u32[]{:S(2)}) async-start(bf16[16,128,128]{2,1,0:T(8,128)(2,1)} %get-tuple-element.31), calls=%async_computation.1 | async-start | bytes 1048576 | tf_op jit(solution)/shard_map/all_to_all | solution.py:503
  101.3 1.1 copy-start.2
  109.9 1.8 copy-start
  111.7 1.6 copy-start.1
  113.3 0.9 copy-start.3
  128.6 23.2 %all-to-all-start.2 = ((bf16[16,128,128]{2,1,0:T(8,128)(2,1)}), bf16[16,128,128]{2,1,0:T(8,128)(2,1)S(1)}, u32[]{:S(2)}, u32[]{:S(2)}) async-start(bf16[16,128,128]{2,1,0:T(8,128)(2,1)} %bitcast.46), calls=%async_computation.2 | async-start | bytes 1048576 | tf_op jit(solution)/shard_map/all_to_all | solution.py:507
  151.8 0.8 copy-start.7
  151.8 13.2 %collective-permute-start.6 = (bf16[8,6,128,128]{3,2,1,0:T(8,128)(2,1)}, bf16[8,6,128,128]{3,2,1,0:T(8,128)(2,1)}, u32[]{:S(2)}, u32[]{:S(2)}) collective-permute-start(bf16[8,6,128,128]{3,2,1,0:T(8,128)(2,1)} %get-tuple-element.41), channel_id=1, source_target_pairs={{0,16},{16,0},{1,17},{17,1},{2,18},{18,2},{3,19},{19,3},{4,20},{20... | collective-permute-start | bytes 4718600 | tf_op jit(solution)/shard_map/ppermute | solution.py:442
  165.0 5.0 %copy-start.8 = (bf16[8,6,128,128]{3,2,1,0:T(8,128)(2,1)S(1)}, bf16[8,6,128,128]{3,2,1,0:T(8,128)(2,1)}, u32[]{:S(2)}) copy-start(bf16[8,6,128,128]{3,2,1,0:T(8,128)(2,1)} %get-tuple-element.48) | copy-start | bytes 4718596
  165.0 47.1 %all-to-all-start.3 = ((bf16[16,3,128,128]{3,2,1,0:T(8,128)(2,1)}), bf16[16,3,128,128]{3,2,1,0:T(8,128)(2,1)S(1)}, u32[]{:S(2)}, u32[]{:S(2)}) async-start(bf16[16,3,128,128]{3,2,1,0:T(8,128)(2,1)} %attend_back.1), calls=%async_computation.3 | async-start | bytes 3145728 | tf_op jit(solution)/shard_map/all_to_all | solution.py:515
  171.4 19.0 %collective-permute-start.7 = (bf16[2,6,128,128]{3,2,1,0:T(8,128)(2,1)S(1)}, bf16[2,6,128,128]{3,2,1,0:T(8,128)(2,1)S(1)}, u32[]{:S(2)}, u32[]{:S(2)}) collective-permute-start(bf16[2,6,128,128]{3,2,1,0:T(8,128)(2,1)S(1)} %get-tuple-element.57), channel_id=1, source_target_pairs={{0,128},{128,8},{8,136},{136,0},{1,129},{129,9},{9,137},{137,1},{2... | collective-permute-start | bytes 1179656 | tf_op jit(solution)/shard_map/ppermute | solution.py:453
  172.3 18.1 %collective-permute-start.8 = (bf16[2,6,128,128]{3,2,1,0:T(8,128)(2,1)S(1)}, bf16[2,6,128,128]{3,2,1,0:T(8,128)(2,1)S(1)}, u32[]{:S(2)}, u32[]{:S(2)}) collective-permute-start(bf16[2,6,128,128]{3,2,1,0:T(8,128)(2,1)S(1)} %get-tuple-element.58), channel_id=1, source_target_pairs={{0,136},{128,0},{8,128},{136,8},{1,137},{129,1},{9,129},{137,9},{2... | collective-permute-start | bytes 1179656 | tf_op jit(solution)/shard_map/ppermute | solution.py:453
  192.0 7.9 %collective-permute-start.10 = (bf16[6,128,128]{2,1,0:T(8,128)(2,1)S(1)}, bf16[6,128,128]{2,1,0:T(8,128)(2,1)S(1)}, u32[]{:S(2)}, u32[]{:S(2)}) collective-permute-start(bf16[6,128,128]{2,1,0:T(8,128)(2,1)S(1)} %get-tuple-element.56), channel_id=1, source_target_pairs={{0,32},{32,64},{64,96},{96,0},{1,33},{33,65},{65,97},{97,1},{2,34}... | collective-permute-start | bytes 589832 | tf_op jit(solution)/shard_map/ppermute | solution.py:447
  192.9 11.8 %collective-permute-start.11 = (bf16[6,128,128]{2,1,0:T(8,128)(2,1)S(1)}, bf16[6,128,128]{2,1,0:T(8,128)(2,1)S(1)}, u32[]{:S(2)}, u32[]{:S(2)}) collective-permute-start(bf16[6,128,128]{2,1,0:T(8,128)(2,1)S(1)} %get-tuple-element.55), channel_id=1, source_target_pairs={{0,96},{32,0},{64,32},{96,64},{1,97},{33,1},{65,33},{97,65},{2,98}... | collective-permute-start | bytes 589832 | tf_op jit(solution)/shard_map/ppermute | solution.py:447
  194.1 10.5 %collective-permute-start.9 = (bf16[6,128,128]{2,1,0:T(8,128)(2,1)S(1)}, bf16[6,128,128]{2,1,0:T(8,128)(2,1)S(1)}, u32[]{:S(2)}, u32[]{:S(2)}) collective-permute-start(bf16[6,128,128]{2,1,0:T(8,128)(2,1)S(1)} %get-tuple-element.54), channel_id=1, source_target_pairs={{0,64},{32,96},{64,0},{96,32},{1,65},{33,97},{65,1},{97,33},{2,66}... | collective-permute-start | bytes 589832 | tf_op jit(solution)/shard_map/ppermute | solution.py:447
  204.8 7.3 %collective-permute-start.12 = (bf16[6,128,128]{2,1,0:T(8,128)(2,1)S(1)}, bf16[6,128,128]{2,1,0:T(8,128)(2,1)S(1)}, u32[]{:S(2)}, u32[]{:S(2)}) collective-permute-start(bf16[6,128,128]{2,1,0:T(8,128)(2,1)S(1)} %fusion.2), channel_id=1, source_target_pairs={{0,8},{8,0},{1,9},{9,1},{2,10},{10,2},{3,11},{11,3},{4,12},{12,4},... | collective-permute-start | bytes 589832 | tf_op jit(solution)/shard_map/ppermute | solution.py:462
  229.6 13.1 %all-to-all-start.5 = ((bf16[8,96,128]{2,1,0:T(8,128)(2,1)}), bf16[8,96,128]{2,1,0:T(8,128)(2,1)S(1)}, u32[]{:S(2)}, u32[]{:S(2)}) async-start(bf16[8,96,128]{2,1,0:T(8,128)(2,1)} %broadcast_in_dim.14), calls=%async_computation.5 | async-start | bytes 393216 | tf_op jit(solution)/shard_map/all_to_all | solution.py:527
Sparse Core Ops, SparseCore 0:
  9.8 102.6 all-gather.1

commit v3 on v2

--- a/solution.py
+++ b/solution.py
@@ -471,7 +471,10 @@
 
 
 def gather_column(own):
-    return jnp.concatenate([own, shift(own, "y", 1), shift(own, "y", 3), shift(own, "y", 2)], axis=0)
+    half = own.shape[0] // 2
+    before, behind = shift(own, "y", 1), shift(own, "y", 3)
+    across = [shift(before[:half], "y", 1), shift(behind[half:], "y", 3)]
+    return jnp.concatenate([own, before, behind] + across, axis=0)
 
 
 def gather_blocks(column, crossed):
@@ -517,14 +520,13 @@
     from_xl = cross(add(mine[4:], from_core[4:]))
     share = add(mine[:4], from_core[:4], from_xl)
     share = add(share[0], *[shift(share[dy], "y", dy) for dy in (2, 1, 3)])
-    share = add(share, partner(share, "xh", 1))
     shape = share.shape
     parts = lax.all_to_all(
-        after(share, grads).reshape(8, -1, BS), "z", split_axis=0, concat_axis=0, tiled=True
+        after(share, grads).reshape(seqs, -1, BS), SEQ, split_axis=0, concat_axis=0, tiled=True
     )
-    part = add(*[parts[i] for i in range(8)])
+    part = add(*[parts[i] for i in range(seqs)])
     copies = jnp.broadcast_to(part[None], parts.shape)
-    owner_grad = lax.all_to_all(copies, "z", split_axis=0, concat_axis=0, tiled=True).reshape(shape)
+    owner_grad = lax.all_to_all(copies, SEQ, split_axis=0, concat_axis=0, tiled=True).reshape(shape)
     total_tokens = 16 * tok * seqs
     grad_skew = cayley_pullback(inverse, owner_grad, 1.0 / math.sqrt(total_tokens))
     return block_output[None], grad_inputs, grad_skew

time: 253 us -> 251 us (level)
  waiting for transfers between devices: 82.4 us -> 79.3 us
  starting transfers between devices: 48.6 us -> 51.7 us
    ppermute x1 -> x0, waiting for transfers between devices: 7.1 us -> none  [partner(): lax.ppermute(x, axis, [(i, i ^ bit) for i in range(lax.axis_size(axis))])]
    all_to_all x1, waiting for transfers between devices: 0.01 us -> 5.32 us  [local(): grads = lax.all_to_all(grads, SEQ, split_axis=0, concat_axis=0, tiled=True)]
    all_to_all x1, starting transfers between devices: 5.84 us -> 8.85 us  [local(): lax.all_to_all(grad_att.reshape(seqs, HD, tok), SEQ, split_axis=0, concat...]
    ppermute x6 -> x7, waiting for transfers between devices: 25.9 us -> 23.7 us  [shift(): return lax.ppermute(x, axis, [(i, (i + by) % n) for i in range(n)])]
    ppermute x6 -> x7, starting transfers between devices: 6.38 us -> 6.46 us  [shift(): return lax.ppermute(x, axis, [(i, (i + by) % n) for i in range(n)])]
    unnamed x24 -> x25, local copies, waits for them, and re-layouts: 12 us -> 11.9 us
  transfers between devices with their start and end apart: 19 -> 19, of which waited for: 11 -> 12; matrix products, arithmetic and copies ran while one was open for 5% -> 5% of each run, Pallas kernels for 22% -> 22%
where the time goes in v3:
time: 251 us; the launch traced here: 250 us
  waiting for transfers between devices  79.3 us (32%)
  Pallas kernels  67.6 us (27%)
  starting transfers between devices  51.7 us (21%)
  local copies, waits for them, and re-layouts  17.2 us (7%)
  blocking collectives  15.2 us (6%)
  between operations  14.3 us (6%)
  other arithmetic  4.66 us (2%)
    ppermute x4, waiting for transfers between devices, turn(): lax.ppermute(x, ('xl', 'xh'), [(at[i], at[(i + by) % 4]) for i in range(4)])  32.6 us
    ppermute x7, waiting for transfers between devices, shift(): return lax.ppermute(x, axis, [(i, (i + by) % n) for i in range(n)])  23.7 us
    all_to_all x1, blocking collectives, local(): lax.all_to_all(after(share, grads).reshape(seqs, -1, BS), SEQ, split_axis...  15.2 us
    pallas_call x1, Pallas kernels, cayley(): pl.pallas_call(inverse_kernel, out_shape=(jax.ShapeDtypeStruct(skew.shape...  14 us
    pallas_call x1, Pallas kernels, attend_back(): pl.pallas_call(attend_back_kernel, grid=(steps,), in_specs=[pl.BlockSpec(...  12.4 us
    unnamed x25, local copies, waits for them, and re-layouts  11.9 us
    pallas_call x1, Pallas kernels, attend(): pl.pallas_call(attend_kernel, grid=(steps,), in_specs=[pl.BlockSpec((per,...  11.4 us
    all_to_all x1, starting transfers between devices, local(): spread = lax.all_to_all(rows, SEQ, split_axis=0, concat_axis=0, tiled=True)  11.2 us
  transfers between devices with their start and end apart: 19, of which 12 were waited for; matrix products, arithmetic and copies ran while one was open for 5% of the time, Pallas kernels for 22%

profile of v3, /device:TPU:24, one launch (start us, length us, event | category | flops | bytes accessed | tf_op | source)
XLA Modules:
  0.0 250.0 jit_solution(2758519333446363404)
XLA Ops:
  7.2 0.7 all-gather.2.cloned.1.call-update
  7.9 1.9 copy.9
  9.8 1.6 copy.10
  11.4 11.2 %all-to-all-start = ((bf16[16,3,128,128]{3,2,1,0:T(8,128)(2,1)}), bf16[16,3,128,128]{3,2,1,0:T(8,128)(2,1)S(1)}, u32[]{:S(2)}, u32[]{:S(2)}) async-start(bf16[16,3,128,128]{3,2,1,0:T(8,128)(2,1)} %bitcast.42), calls=%async_computation | async-start | bytes 3145728 | tf_op jit(solution)/shard_map/all_to_all | solution.py:500
  22.6 14.0 %cayley.1 = (f32[6,128,128]{2,1,0:T(8,128)S(1)}, bf16[6,128,128]{2,1,0:T(8,128)(2,1)S(1)}) custom-call(f32[6,128,128]{2,1,0:T(8,128)S(1)} %copy-done.4), custom_call_target="tpu_custom_call" | custom-call | tf_op jit(solution)/shard_map/cayley/pallas_call | solution.py:75
  36.9 1.8 collective-permute-start.1
  38.7 9.4 %collective-permute-done = bf16[6,128,128]{2,1,0:T(8,128)(2,1)S(1)} collective-permute-done((bf16[6,128,128]{2,1,0:T(8,128)(2,1)S(1)}, bf16[6,128,128]{2,1,0:T(8,128)(2,1)S(1)}, u32[]{:S(2)}, u32[]{:S(2)}) %collective-permute-start) | collective-permute-done | bytes 196640 | tf_op jit(solution)/shard_map/ppermute | solution.py:447
  48.3 2.1 collective-permute-start.3
  50.4 0.7 collective-permute-start.4
  51.1 4.2 %collective-permute-done.2 = bf16[3,128,128]{2,1,0:T(8,128)(2,1)S(1)} collective-permute-done((bf16[3,128,128]{2,1,0:T(8,128)(2,1)S(1)}, bf16[3,128,128]{2,1,0:T(8,128)(2,1)S(1)}, u32[]{:S(2)}, u32[]{:S(2)}) %collective-permute-start.2) | collective-permute-done | bytes 98336 | tf_op jit(solution)/shard_map/ppermute | solution.py:447
  55.3 3.1 %collective-permute-start.5 = (bf16[12,128,128]{2,1,0:T(8,128)(2,1)S(1)}, bf16[12,128,128]{2,1,0:T(8,128)(2,1)S(1)}, u32[]{:S(2)}, u32[]{:S(2)}) collective-permute-start(bf16[12,128,128]{2,1,0:T(8,128)(2,1)S(1)} %pad_maximum_fusion.2), channel_id=1, source_target_pairs={{0,136},{128,0},{8,128},{136,8},{1,137},{129,1},{9,129},{137,9},{2... | collective-permute-start | bytes 1179656 | tf_op jit(solution)/shard_map/ppermute | solution.py:453
  58.5 11.7 %collective-permute-done.4 = bf16[12,128,128]{2,1,0:T(8,128)(2,1)S(1)} collective-permute-done((bf16[12,128,128]{2,1,0:T(8,128)(2,1)S(1)}, bf16[12,128,128]{2,1,0:T(8,128)(2,1)S(1)}, u32[]{:S(2)}, u32[]{:S(2)}) %collective-permute-start.4) | collective-permute-done | bytes 393248 | tf_op jit(solution)/shard_map/ppermute | solution.py:453
  70.1 5.3 %collective-permute-done.5 = bf16[12,128,128]{2,1,0:T(8,128)(2,1)S(1)} collective-permute-done((bf16[12,128,128]{2,1,0:T(8,128)(2,1)S(1)}, bf16[12,128,128]{2,1,0:T(8,128)(2,1)S(1)}, u32[]{:S(2)}, u32[]{:S(2)}) %collective-permute-start.5) | collective-permute-done | bytes 393248 | tf_op jit(solution)/shard_map/ppermute | solution.py:453
  75.4 0.9 pad_maximum_fusion
  76.4 1.1 copy-done.6
  77.5 1.3 constant_dynamic-update-slice_fusion.near_ref
  78.9 11.4 %attend.1 = (bf16[16,128,128]{2,1,0:T(8,128)(2,1)}, f32[4,128,512]{2,1,0:T(8,128)}, bf16[4,2048,512]{2,1,0:T(8,128)(2,1)}, f32[4,1,512]{2,1,0:T(1,128)}) custom-call(bf16[16,3,128,128]{3,2,1,0:T(8,128)(2,1)} %copy-done.6, bf16[16,3,128,128]{3,2,1,0:T(8,128)(2,1)} %copy-done.6, bf16[16,3,128,128]{3,2,1,0:T(8,128)(2,1)} %copy-done.6), custom_call_target="tpu_custom_call" | custom-call | flops 2147483648 | bytes 8388608 | tf_op jit(solution)/shard_map/attend/pallas_call | solution.py:139
  90.3 8.7 %all-to-all-start.1 = ((bf16[16,128,128]{2,1,0:T(8,128)(2,1)}), bf16[16,128,128]{2,1,0:T(8,128)(2,1)}, u32[]{:S(2)}, u32[]{:S(2)}) async-start(bf16[16,128,128]{2,1,0:T(8,128)(2,1)} %get-tuple-element.31), calls=%async_computation.1 | async-start | bytes 1048576 | tf_op jit(solution)/shard_map/all_to_all | solution.py:506
  99.0 1.1 copy-done.2
  100.2 7.5 %butterfly_down.1 = (bf16[4,3072,128]{2,1,0:T(8,128)(2,1)S(1)}, bf16[3072,128]{1,0:T(8,128)(2,1)S(1)}, bf16[96,128,128]{2,1,0:T(8,128)(2,1)S(1)}) custom-call(s32[4,96]{1,0:T(4,128)S(1)} %copy-done.5, s32[96]{0:T(128)S(1)} %fusion.4.home_ref, bf16[128,3072]{1,0:T(8,128)(2,1)S(1)} %bitcast.40, ...), custom_call_target="tpu_custom_call" | custom-call | flops 1000000000 | bytes 10000000 | tf_op jit(solution)/shard_map/butterfly_down/pallas_call | solution.py:292
  107.7 1.8 copy-done
  109.4 1.6 copy-done.1
  111.1 0.9 copy-done.3
  111.9 4.6 %all-to-all-done.1.att_ref = bf16[16,128,128]{2,1,0:T(8,128)(2,1)} async-done(((bf16[16,128,128]{2,1,0:T(8,128)(2,1)}), bf16[16,128,128]{2,1,0:T(8,128)(2,1)}, u32[]{:S(2)}, u32[]{:S(2)}) %all-to-all-start.1) | async-done | bytes 524320 | tf_op jit(solution)/shard_map/all_to_all | solution.py:506
  116.5 9.8 %products.1 = (bf16[2048,128]{1,0:T(8,128)(2,1)}, bf16[128,3072]{1,0:T(8,128)(2,1)}) custom-call(bf16[2048,3072]{1,0:T(8,128)(2,1)} %all-gather.2.cloned.1.call-done.weight_ref, bf16[3072,128]{1,0:T(8,128)(2,1)} %copy-done.3, bf16[16,128,128]{2,1,0:T(8,128)(2,1)} %all-to-all-done.1.att_ref), custom_call_target="tpu_custom_call" | custom-call | flops 3221225472 | bytes 12582912 | tf_op jit(solution)/shard_map/products/pallas_call | solution.py:416
  126.3 8.8 %all-to-all-start.2 = ((bf16[16,128,128]{2,1,0:T(8,128)(2,1)}), bf16[16,128,128]{2,1,0:T(8,128)(2,1)S(1)}, u32[]{:S(2)}, u32[]{:S(2)}) async-start(bf16[16,128,128]{2,1,0:T(8,128)(2,1)} %bitcast.46), calls=%async_computation.2 | async-start | bytes 1048576 | tf_op jit(solution)/shard_map/all_to_all | solution.py:510
  135.2 0.6 pad_add_fusion.self_ref
  135.7 10.7 %butterfly_up.1 = (bf16[128,3072]{1,0:T(8,128)(2,1)}, bf16[8,6,128,128]{3,2,1,0:T(8,128)(2,1)}, bf16[8,6,128,128]{3,2,1,0:T(8,128)(2,1)}) custom-call(s32[4,96]{1,0:T(4,128)} %order_ref.3, s32[3]{0:T(128)} %pad_add_fusion.self_ref, bf16[128,3072]{1,0:T(8,128)(2,1)} %get-tuple-element.34.proj_ref, bf16[96,128,128]{2,1,0:T(8,128)(2,1)} %copy-done.1, ...), custom_call_target="tpu_custom_call" | custom-call | flops 1000000000 | bytes 10000000 | tf_op jit(solution)/shard_map/butterfly_up/pallas_call | solution.py:368
  146.4 6.1 %all-to-all-done.2.dout_ref = bf16[16,128,128]{2,1,0:T(8,128)(2,1)S(1)} async-done(((bf16[16,128,128]{2,1,0:T(8,128)(2,1)}), bf16[16,128,128]{2,1,0:T(8,128)(2,1)S(1)}, u32[]{:S(2)}, u32[]{:S(2)}) %all-to-all-start.2) | async-done | bytes 524320 | tf_op jit(solution)/shard_map/all_to_all | solution.py:510
  152.6 0.8 copy-done.7
  153.3 12.4 %attend_back.1 = bf16[16,3,128,128]{3,2,1,0:T(8,128)(2,1)} custom-call(bf16[16,3,128,128]{3,2,1,0:T(8,128)(2,1)} %copy-done.6, bf16[16,3,128,128]{3,2,1,0:T(8,128)(2,1)} %copy-done.6, bf16[16,3,128,128]{3,2,1,0:T(8,128)(2,1)} %copy-done.6, bf16[16,128,128]{2,1,0:T(8,128)(2,1)} %copy-done.7, f32[4,128,512]{2,1,0:T(8,128)} %get-tuple-element.43.wide_ref, ...), custom_call_target="tpu_custom_call" | custom-call | flops 4294967296 | bytes 8388608 | tf_op jit(solution)/shard_map/attend_back/pallas_call | solution.py:213
  165.8 5.0 %all-to-all-start.3 = ((bf16[16,3,128,128]{3,2,1,0:T(8,128)(2,1)}), bf16[16,3,128,128]{3,2,1,0:T(8,128)(2,1)S(1)}, u32[]{:S(2)}, u32[]{:S(2)}) async-start(bf16[16,3,128,128]{3,2,1,0:T(8,128)(2,1)} %attend_back.1), calls=%async_computation.3 | async-start | bytes 3145728 | tf_op jit(solution)/shard_map/all_to_all | solution.py:518
  170.7 1.4 add_convert_fusion.1
  172.3 3.2 %collective-permute-start.9 = (bf16[2,6,128,128]{3,2,1,0:T(8,128)(2,1)S(1)}, bf16[2,6,128,128]{3,2,1,0:T(8,128)(2,1)S(1)}, u32[]{:S(2)}, u32[]{:S(2)}) collective-permute-start(bf16[2,6,128,128]{3,2,1,0:T(8,128)(2,1)S(1)} %get-tuple-element.58), channel_id=1, source_target_pairs={{0,136},{128,0},{8,128},{136,8},{1,137},{129,1},{9,129},{137,9},{2... | collective-permute-start | bytes 1179656 | tf_op jit(solution)/shard_map/ppermute | solution.py:453
  175.5 15.7 %collective-permute-done.8 = bf16[2,6,128,128]{3,2,1,0:T(8,128)(2,1)S(1)} collective-permute-done((bf16[2,6,128,128]{3,2,1,0:T(8,128)(2,1)S(1)}, bf16[2,6,128,128]{3,2,1,0:T(8,128)(2,1)S(1)}, u32[]{:S(2)}, u32[]{:S(2)}) %collective-permute-start.8) | collective-permute-done | bytes 393248 | tf_op jit(solution)/shard_map/ppermute | solution.py:453
  191.2 1.5 add_convert_fusion
  193.0 2.0 collective-permute-start.12
  194.9 7.2 %collective-permute-done.10 = bf16[6,128,128]{2,1,0:T(8,128)(2,1)S(1)} collective-permute-done((bf16[6,128,128]{2,1,0:T(8,128)(2,1)S(1)}, bf16[6,128,128]{2,1,0:T(8,128)(2,1)S(1)}, u32[]{:S(2)}, u32[]{:S(2)}) %collective-permute-start.10) | collective-permute-done | bytes 196640 | tf_op jit(solution)/shard_map/ppermute | solution.py:447
  202.2 0.4 collective-permute-done.11
  202.6 2.5 collective-permute-done.12
  205.2 5.3 %all-to-all-done.3 = bf16[16,3,128,128]{3,2,1,0:T(8,128)(2,1)S(1)} async-done(((bf16[16,3,128,128]{3,2,1,0:T(8,128)(2,1)}), bf16[16,3,128,128]{3,2,1,0:T(8,128)(2,1)S(1)}, u32[]{:S(2)}, u32[]{:S(2)}) %all-to-all-start.3) | async-done | bytes 1572896 | tf_op jit(solution)/shard_map/all_to_all | solution.py:518
  210.5 15.2 %all_to_all.30 = bf16[16,48,128]{2,1,0:T(8,128)(2,1)S(1)} all-to-all(bf16[16,48,128]{2,1,0:T(8,128)(2,1)S(1)} %bitcast.45), channel_id=1, replica_groups=mesh['xl'=2,'y'=4,'c'=2,'xh'=2,'z'=8] {'xh','z'}, dimensions={0} | all-to-all | bytes 393216 | tf_op jit(solution)/shard_map/all_to_all | solution.py:524
  225.7 0.7 broadcast_in_dim.14
  226.4 4.4 %all-to-all-start.5 = ((bf16[16,48,128]{2,1,0:T(8,128)(2,1)}), bf16[16,48,128]{2,1,0:T(8,128)(2,1)S(1)}, u32[]{:S(2)}, u32[]{:S(2)}) async-start(bf16[16,48,128]{2,1,0:T(8,128)(2,1)} %broadcast_in_dim.14), calls=%async_computation.5 | async-start | bytes 393216 | tf_op jit(solution)/shard_map/all_to_all | solution.py:529
  230.8 1.6 copy.11
  232.4 2.6 %copy.12 = bf16[1,128,3,2048]{3,1,2,0:T(8,128)(2,1)} copy(bf16[1,128,3,2048]{1,3,2,0:T(8,128)(2,1)} %bitcast.43) | data formatting | bytes 3145728
  235.0 6.3 %all-to-all-done.5 = bf16[16,48,128]{2,1,0:T(8,128)(2,1)S(1)} async-done(((bf16[16,48,128]{2,1,0:T(8,128)(2,1)}), bf16[16,48,128]{2,1,0:T(8,128)(2,1)S(1)}, u32[]{:S(2)}, u32[]{:S(2)}) %all-to-all-start.5) | async-done | bytes 196640 | tf_op jit(solution)/shard_map/all_to_all | solution.py:529
  241.3 1.9 cayley_pullback.1
  (41 shorter events, 1.4 us)
Async XLA Ops:
  7.2 109.4 %all-gather.2.cloned.1.call-start = ((), (), s32[]{:S(2)}) async-start(), calls=%async_computation.6 | async-start | bytes 13369344 | tf_op jit(solution)/shard_map/all_gather | solution.py:498
  11.4 11.2 %copy-start.4 = (f32[6,128,128]{2,1,0:T(8,128)S(1)}, f32[6,128,128]{2,1,0:T(8,128)}, u32[]{:S(2)}) copy-start(f32[6,128,128]{2,1,0:T(8,128)} %skew_ref) | copy-start | bytes 1179652
  11.4 65.0 %all-to-all-start = ((bf16[16,3,128,128]{3,2,1,0:T(8,128)(2,1)}), bf16[16,3,128,128]{3,2,1,0:T(8,128)(2,1)S(1)}, u32[]{:S(2)}, u32[]{:S(2)}) async-start(bf16[16,3,128,128]{3,2,1,0:T(8,128)(2,1)} %bitcast.42), calls=%async_computation | async-start | bytes 3145728 | tf_op jit(solution)/shard_map/all_to_all | solution.py:500
  36.6 11.6 %collective-permute-start = (bf16[6,128,128]{2,1,0:T(8,128)(2,1)S(1)}, bf16[6,128,128]{2,1,0:T(8,128)(2,1)S(1)}, u32[]{:S(2)}, u32[]{:S(2)}) collective-permute-start(bf16[6,128,128]{2,1,0:T(8,128)(2,1)S(1)} %get-tuple-element.28), channel_id=1, source_target_pairs={{0,32},{32,64},{64,96},{96,0},{1,33},{33,65},{65,97},{97,1},{2,34}... | collective-permute-start | bytes 589832 | tf_op jit(solution)/shard_map/ppermute | solution.py:447
  36.9 11.4 %collective-permute-start.1 = (bf16[6,128,128]{2,1,0:T(8,128)(2,1)S(1)}, bf16[6,128,128]{2,1,0:T(8,128)(2,1)S(1)}, u32[]{:S(2)}, u32[]{:S(2)}) collective-permute-start(bf16[6,128,128]{2,1,0:T(8,128)(2,1)S(1)} %get-tuple-element.28), channel_id=1, source_target_pairs={{0,96},{32,0},{64,32},{96,64},{1,97},{33,1},{65,33},{97,65},{2,98}... | collective-permute-start | bytes 589832 | tf_op jit(solution)/shard_map/ppermute | solution.py:447
  48.2 7.1 %collective-permute-start.2 = (bf16[3,128,128]{2,1,0:T(8,128)(2,1)S(1)}, bf16[3,128,128]{2,1,0:T(8,128)(2,1)S(1)}, u32[]{:S(2)}, u32[]{:S(2)}) collective-permute-start(bf16[3,128,128]{2,1,0:T(8,128)(2,1)S(1)} %slice.121), channel_id=1, source_target_pairs={{0,32},{32,64},{64,96},{96,0},{1,33},{33,65},{65,97},{97,1},{2,34}... | collective-permute-start | bytes 294920 | tf_op jit(solution)/shard_map/ppermute | solution.py:447
  48.3 7.0 %collective-permute-start.3 = (bf16[3,128,128]{2,1,0:T(8,128)(2,1)S(1)}, bf16[3,128,128]{2,1,0:T(8,128)(2,1)S(1)}, u32[]{:S(2)}, u32[]{:S(2)}) collective-permute-start(bf16[3,128,128]{2,1,0:T(8,128)(2,1)S(1)} %slice.122), channel_id=1, source_target_pairs={{0,96},{32,0},{64,32},{96,64},{1,97},{33,1},{65,33},{97,65},{2,98}... | collective-permute-start | bytes 294920 | tf_op jit(solution)/shard_map/ppermute | solution.py:447
  50.4 19.7 %collective-permute-start.4 = (bf16[12,128,128]{2,1,0:T(8,128)(2,1)S(1)}, bf16[12,128,128]{2,1,0:T(8,128)(2,1)S(1)}, u32[]{:S(2)}, u32[]{:S(2)}) collective-permute-start(bf16[12,128,128]{2,1,0:T(8,128)(2,1)S(1)} %pad_maximum_fusion.1), channel_id=1, source_target_pairs={{0,128},{128,8},{8,136},{136,0},{1,129},{129,9},{9,137},{137,1},{2... | collective-permute-start | bytes 1179656 | tf_op jit(solution)/shard_map/ppermute | solution.py:453
  55.3 20.1 %collective-permute-start.5 = (bf16[12,128,128]{2,1,0:T(8,128)(2,1)S(1)}, bf16[12,128,128]{2,1,0:T(8,128)(2,1)S(1)}, u32[]{:S(2)}, u32[]{:S(2)}) collective-permute-start(bf16[12,128,128]{2,1,0:T(8,128)(2,1)S(1)} %pad_maximum_fusion.2), channel_id=1, source_target_pairs={{0,136},{128,0},{8,128},{136,8},{1,137},{129,1},{9,129},{137,9},{2... | collective-permute-start | bytes 1179656 | tf_op jit(solution)/shard_map/ppermute | solution.py:453
  76.4 1.1 copy-start.6
  78.8 20.2 %copy-start.5 = (s32[4,96]{1,0:T(4,128)S(1)}, s32[4,96]{1,0:T(4,128)}, u32[]{:S(2)}) copy-start(s32[4,96]{1,0:T(4,128)} %order_ref.3) | copy-start | bytes 4612
  78.8 20.2 %collective-permute-start.6 = (bf16[48,128,128]{2,1,0:T(8,128)(2,1)S(1)}, bf16[48,128,128]{2,1,0:T(8,128)(2,1)S(1)}, u32[]{:S(2)}, u32[]{:S(2)}) collective-permute-start(bf16[48,128,128]{2,1,0:T(8,128)(2,1)S(1)} %constant_dynamic-update-slice_fusion.near_ref), channel_id=1, source_target_pairs={{0,16},{16,0},{1,17},{17,1},{2,18},{18,2},{3,19},{19,3},{4,20},{20... | collective-permute-start | bytes 4718600 | tf_op jit(solution)/shard_map/ppermute | solution.py:442
  90.3 26.3 %all-to-all-start.1 = ((bf16[16,128,128]{2,1,0:T(8,128)(2,1)}), bf16[16,128,128]{2,1,0:T(8,128)(2,1)}, u32[]{:S(2)}, u32[]{:S(2)}) async-start(bf16[16,128,128]{2,1,0:T(8,128)(2,1)} %get-tuple-element.31), calls=%async_computation.1 | async-start | bytes 1048576 | tf_op jit(solution)/shard_map/all_to_all | solution.py:506
  99.0 1.1 copy-start.2
  107.7 1.8 copy-start
  109.4 1.6 copy-start.1
  111.1 0.9 copy-start.3
  126.3 26.2 %all-to-all-start.2 = ((bf16[16,128,128]{2,1,0:T(8,128)(2,1)}), bf16[16,128,128]{2,1,0:T(8,128)(2,1)S(1)}, u32[]{:S(2)}, u32[]{:S(2)}) async-start(bf16[16,128,128]{2,1,0:T(8,128)(2,1)} %bitcast.46), calls=%async_computation.2 | async-start | bytes 1048576 | tf_op jit(solution)/shard_map/all_to_all | solution.py:510
  152.5 0.8 copy-start.7
  152.5 13.2 %collective-permute-start.7 = (bf16[8,6,128,128]{3,2,1,0:T(8,128)(2,1)}, bf16[8,6,128,128]{3,2,1,0:T(8,128)(2,1)}, u32[]{:S(2)}, u32[]{:S(2)}) collective-permute-start(bf16[8,6,128,128]{3,2,1,0:T(8,128)(2,1)} %get-tuple-element.41), channel_id=1, source_target_pairs={{0,16},{16,0},{1,17},{17,1},{2,18},{18,2},{3,19},{19,3},{4,20},{20... | collective-permute-start | bytes 4718600 | tf_op jit(solution)/shard_map/ppermute | solution.py:442
  165.7 5.0 %copy-start.8 = (bf16[8,6,128,128]{3,2,1,0:T(8,128)(2,1)S(1)}, bf16[8,6,128,128]{3,2,1,0:T(8,128)(2,1)}, u32[]{:S(2)}) copy-start(bf16[8,6,128,128]{3,2,1,0:T(8,128)(2,1)} %get-tuple-element.48) | copy-start | bytes 4718596
  165.8 44.7 %all-to-all-start.3 = ((bf16[16,3,128,128]{3,2,1,0:T(8,128)(2,1)}), bf16[16,3,128,128]{3,2,1,0:T(8,128)(2,1)S(1)}, u32[]{:S(2)}, u32[]{:S(2)}) async-start(bf16[16,3,128,128]{3,2,1,0:T(8,128)(2,1)} %attend_back.1), calls=%async_computation.3 | async-start | bytes 3145728 | tf_op jit(solution)/shard_map/all_to_all | solution.py:518
  172.2 19.0 %collective-permute-start.8 = (bf16[2,6,128,128]{3,2,1,0:T(8,128)(2,1)S(1)}, bf16[2,6,128,128]{3,2,1,0:T(8,128)(2,1)S(1)}, u32[]{:S(2)}, u32[]{:S(2)}) collective-permute-start(bf16[2,6,128,128]{3,2,1,0:T(8,128)(2,1)S(1)} %get-tuple-element.57), channel_id=1, source_target_pairs={{0,128},{128,8},{8,136},{136,0},{1,129},{129,9},{9,137},{137,1},{2... | collective-permute-start | bytes 1179656 | tf_op jit(solution)/shard_map/ppermute | solution.py:453
  172.3 18.8 %collective-permute-start.9 = (bf16[2,6,128,128]{3,2,1,0:T(8,128)(2,1)S(1)}, bf16[2,6,128,128]{3,2,1,0:T(8,128)(2,1)S(1)}, u32[]{:S(2)}, u32[]{:S(2)}) collective-permute-start(bf16[2,6,128,128]{3,2,1,0:T(8,128)(2,1)S(1)} %get-tuple-element.58), channel_id=1, source_target_pairs={{0,136},{128,0},{8,128},{136,8},{1,137},{129,1},{9,129},{137,9},{2... | collective-permute-start | bytes 1179656 | tf_op jit(solution)/shard_map/ppermute | solution.py:453
  192.7 9.4 %collective-permute-start.10 = (bf16[6,128,128]{2,1,0:T(8,128)(2,1)S(1)}, bf16[6,128,128]{2,1,0:T(8,128)(2,1)S(1)}, u32[]{:S(2)}, u32[]{:S(2)}) collective-permute-start(bf16[6,128,128]{2,1,0:T(8,128)(2,1)S(1)} %get-tuple-element.54), channel_id=1, source_target_pairs={{0,64},{32,96},{64,0},{96,32},{1,65},{33,97},{65,1},{97,33},{2,66}... | collective-permute-start | bytes 589832 | tf_op jit(solution)/shard_map/ppermute | solution.py:447
  192.8 9.8 %collective-permute-start.11 = (bf16[6,128,128]{2,1,0:T(8,128)(2,1)S(1)}, bf16[6,128,128]{2,1,0:T(8,128)(2,1)S(1)}, u32[]{:S(2)}, u32[]{:S(2)}) collective-permute-start(bf16[6,128,128]{2,1,0:T(8,128)(2,1)S(1)} %get-tuple-element.56), channel_id=1, source_target_pairs={{0,32},{32,64},{64,96},{96,0},{1,33},{33,65},{65,97},{97,1},{2,34}... | collective-permute-start | bytes 589832 | tf_op jit(solution)/shard_map/ppermute | solution.py:447
  193.0 12.1 %collective-permute-start.12 = (bf16[6,128,128]{2,1,0:T(8,128)(2,1)S(1)}, bf16[6,128,128]{2,1,0:T(8,128)(2,1)S(1)}, u32[]{:S(2)}, u32[]{:S(2)}) collective-permute-start(bf16[6,128,128]{2,1,0:T(8,128)(2,1)S(1)} %get-tuple-element.55), channel_id=1, source_target_pairs={{0,96},{32,0},{64,32},{96,64},{1,97},{33,1},{65,33},{97,65},{2,98}... | collective-permute-start | bytes 589832 | tf_op jit(solution)/shard_map/ppermute | solution.py:447
  226.4 14.8 %all-to-all-start.5 = ((bf16[16,48,128]{2,1,0:T(8,128)(2,1)}), bf16[16,48,128]{2,1,0:T(8,128)(2,1)S(1)}, u32[]{:S(2)}, u32[]{:S(2)}) async-start(bf16[16,48,128]{2,1,0:T(8,128)(2,1)} %broadcast_in_dim.14), calls=%async_computation.5 | async-start | bytes 393216 | tf_op jit(solution)/shard_map/all_to_all | solution.py:529
Sparse Core Ops, SparseCore 0:
  9.8 105.5 all-gather.1

commit v4 on v3

--- a/solution.py
+++ b/solution.py
@@ -157,7 +157,7 @@
             jax.ShapeDtypeStruct((steps, 1, QB), F32),
         ],
         scratch_shapes=[pltpu.VMEM((HD, length), BF)],
-        compiler_params=params(58, ("arbitrary",)),
+        compiler_params=params(63, ("arbitrary",)),
         cost_estimate=pl.CostEstimate(
             flops=4 * length * length * HD, bytes_accessed=2 * length * length, transcendentals=length * length
         ),
@@ -229,7 +229,7 @@
             pltpu.VMEM((length, HD), F32),
             pltpu.VMEM((length, HD), F32),
         ],
-        compiler_params=params(58, ("arbitrary",)),
+        compiler_params=params(63, ("arbitrary",)),
         cost_estimate=pl.CostEstimate(
             flops=8 * length * length * HD, bytes_accessed=2 * length * length, transcendentals=0
         ),
@@ -383,7 +383,7 @@
             scratch_shapes=[pltpu.VMEM((width, tok), BF), pltpu.VMEM((width, tok), BF)],
         ),
         out_shape=[jax.ShapeDtypeStruct((tok, width), BF), half, half],
-        compiler_params=params(58, ("arbitrary",)),
+        compiler_params=params(63, ("arbitrary",)),
         cost_estimate=pl.CostEstimate(flops=10**9, bytes_accessed=10**7, transcendentals=0),
         name="butterfly_up",
     )(orders, position, projected, flipped, moved.reshape(pairs, rows, tok))
@@ -430,7 +430,7 @@
             jax.ShapeDtypeStruct((tok, width), BF),
         ],
         scratch_shapes=[pltpu.VMEM((tok, width), F32)],
-        compiler_params=params(58, ("arbitrary",)),
+        compiler_params=params(63, ("arbitrary",)),
         cost_estimate=pl.CostEstimate(
             flops=4 * rows * width * tok, bytes_accessed=2 * rows * width, transcendentals=0
         ),

time: 251 us -> 251 us (level)
    ppermute x4, waiting for transfers between devices: 32.6 us -> 30.1 us  [turn(): lax.ppermute(x, ('xl', 'xh'), [(at[i], at[(i + by) % 4]) for i in range(4)])]
    unnamed x25 -> x29, local copies, waits for them, and re-layouts: 11.9 us -> 13.2 us
  transfers between devices with their start and end apart: 19 -> 19, of which waited for: 12 -> 12; matrix products, arithmetic and copies ran while one was open for 5% -> 6% of each run, Pallas kernels for 22% -> 23%
where the time goes in v4:
time: 251 us; the launch traced here: 250 us
  waiting for transfers between devices  77.5 us (31%)
  Pallas kernels  69.1 us (28%)
  starting transfers between devices  52.8 us (21%)
  local copies, waits for them, and re-layouts  17.4 us (7%)
  blocking collectives  15.2 us (6%)
  between operations  14.3 us (6%)
  other arithmetic  3.84 us (2%)
    ppermute x4, waiting for transfers between devices, turn(): lax.ppermute(x, ('xl', 'xh'), [(at[i], at[(i + by) % 4]) for i in range(4)])  30.1 us
    ppermute x7, waiting for transfers between devices, shift(): return lax.ppermute(x, axis, [(i, (i + by) % n) for i in range(n)])  23.1 us
    all_to_all x1, blocking collectives, local(): lax.all_to_all(after(share, grads).reshape(seqs, -1, BS), SEQ, split_axis...  15.2 us
    pallas_call x1, Pallas kernels, cayley(): pl.pallas_call(inverse_kernel, out_shape=(jax.ShapeDtypeStruct(skew.shape...  14 us
    unnamed x29, local copies, waits for them, and re-layouts  13.2 us
    pallas_call x1, Pallas kernels, attend_back(): pl.pallas_call(attend_back_kernel, grid=(steps,), in_specs=[pl.BlockSpec(...  12.4 us
    pallas_call x1, Pallas kernels, attend(): pl.pallas_call(attend_kernel, grid=(steps,), in_specs=[pl.BlockSpec((per,...  11.4 us
    all_to_all x1, starting transfers between devices, local(): spread = lax.all_to_all(rows, SEQ, split_axis=0, concat_axis=0, tiled=True)  11.2 us
  transfers between devices with their start and end apart: 19, of which 12 were waited for; matrix products, arithmetic and copies ran while one was open for 6% of the time, Pallas kernels for 23%

profile of v4, /device:TPU:24, one launch (start us, length us, event | category | flops | bytes accessed | tf_op | source)
XLA Modules:
  0.0 250.1 jit_solution(4196314669981393399)
XLA Ops:
  7.2 0.7 all-gather.2.cloned.1.call-update
  7.9 1.9 copy.9
  9.8 1.6 copy.10
  11.4 11.2 %all-to-all-start = ((bf16[16,3,128,128]{3,2,1,0:T(8,128)(2,1)}), bf16[16,3,128,128]{3,2,1,0:T(8,128)(2,1)S(1)}, u32[]{:S(2)}, u32[]{:S(2)}) async-start(bf16[16,3,128,128]{3,2,1,0:T(8,128)(2,1)} %bitcast.6), calls=%async_computation | async-start | bytes 3145728 | tf_op jit(solution)/shard_map/all_to_all | solution.py:500
  22.6 14.0 %cayley.1 = (f32[6,128,128]{2,1,0:T(8,128)S(1)}, bf16[6,128,128]{2,1,0:T(8,128)(2,1)S(1)}) custom-call(f32[6,128,128]{2,1,0:T(8,128)S(1)} %copy-done.4), custom_call_target="tpu_custom_call" | custom-call | tf_op jit(solution)/shard_map/cayley/pallas_call | solution.py:75
  36.9 1.8 collective-permute-start.1
  38.7 0.7 constant_dynamic-update-slice_fusion.5
  39.4 8.8 %collective-permute-done = bf16[6,128,128]{2,1,0:T(8,128)(2,1)S(1)} collective-permute-done((bf16[6,128,128]{2,1,0:T(8,128)(2,1)S(1)}, bf16[6,128,128]{2,1,0:T(8,128)(2,1)S(1)}, u32[]{:S(2)}, u32[]{:S(2)}) %collective-permute-start) | collective-permute-done | bytes 196640 | tf_op jit(solution)/shard_map/ppermute | solution.py:447
  48.3 2.1 collective-permute-start.3
  50.4 0.7 collective-permute-start.4
  51.1 4.2 %collective-permute-done.2 = bf16[3,128,128]{2,1,0:T(8,128)(2,1)S(1)} collective-permute-done((bf16[3,128,128]{2,1,0:T(8,128)(2,1)S(1)}, bf16[3,128,128]{2,1,0:T(8,128)(2,1)S(1)}, u32[]{:S(2)}, u32[]{:S(2)}) %collective-permute-start.2) | collective-permute-done | bytes 98336 | tf_op jit(solution)/shard_map/ppermute | solution.py:447
  55.3 3.0 %collective-permute-start.5 = (bf16[12,128,128]{2,1,0:T(8,128)(2,1)S(1)}, bf16[12,128,128]{2,1,0:T(8,128)(2,1)S(1)}, u32[]{:S(2)}, u32[]{:S(2)}) collective-permute-start(bf16[12,128,128]{2,1,0:T(8,128)(2,1)S(1)} %pad_maximum_fusion.2), channel_id=1, source_target_pairs={{0,136},{128,0},{8,128},{136,8},{1,137},{129,1},{9,129},{137,9},{2... | collective-permute-start | bytes 1179656 | tf_op jit(solution)/shard_map/ppermute | solution.py:453
  58.4 0.7 constant_dynamic-update-slice_fusion.4
  59.1 0.7 constant_dynamic-update-slice_fusion.3
  59.7 0.6 constant_dynamic-update-slice_fusion.2
  61.0 9.1 %collective-permute-done.4 = bf16[12,128,128]{2,1,0:T(8,128)(2,1)S(1)} collective-permute-done((bf16[12,128,128]{2,1,0:T(8,128)(2,1)S(1)}, bf16[12,128,128]{2,1,0:T(8,128)(2,1)S(1)}, u32[]{:S(2)}, u32[]{:S(2)}) %collective-permute-start.4) | collective-permute-done | bytes 393248 | tf_op jit(solution)/shard_map/ppermute | solution.py:453
  70.1 5.3 %collective-permute-done.5 = bf16[12,128,128]{2,1,0:T(8,128)(2,1)S(1)} collective-permute-done((bf16[12,128,128]{2,1,0:T(8,128)(2,1)S(1)}, bf16[12,128,128]{2,1,0:T(8,128)(2,1)S(1)}, u32[]{:S(2)}, u32[]{:S(2)}) %collective-permute-start.5) | collective-permute-done | bytes 393248 | tf_op jit(solution)/shard_map/ppermute | solution.py:453
  75.5 1.2 copy-done.8
  76.7 0.9 constant_dynamic-update-slice_fusion.near_ref
  77.6 11.4 %attend.1 = (bf16[16,128,128]{2,1,0:T(8,128)(2,1)}, f32[4,128,512]{2,1,0:T(8,128)}, bf16[4,2048,512]{2,1,0:T(8,128)(2,1)}, f32[4,1,512]{2,1,0:T(1,128)}) custom-call(bf16[16,3,128,128]{3,2,1,0:T(8,128)(2,1)} %copy-done.8, bf16[16,3,128,128]{3,2,1,0:T(8,128)(2,1)} %copy-done.8, bf16[16,3,128,128]{3,2,1,0:T(8,128)(2,1)} %copy-done.8), custom_call_target="tpu_custom_call" | custom-call | flops 2147483648 | bytes 8388608 | tf_op jit(solution)/shard_map/attend/pallas_call | solution.py:139
  89.0 8.8 %all-to-all-start.1 = ((bf16[16,128,128]{2,1,0:T(8,128)(2,1)}), bf16[16,128,128]{2,1,0:T(8,128)(2,1)}, u32[]{:S(2)}, u32[]{:S(2)}) async-start(bf16[16,128,128]{2,1,0:T(8,128)(2,1)} %get-tuple-element.31), calls=%async_computation.1 | async-start | bytes 1048576 | tf_op jit(solution)/shard_map/all_to_all | solution.py:506
  97.9 8.9 %butterfly_down.1 = (bf16[4,3072,128]{2,1,0:T(8,128)(2,1)S(1)}, bf16[3072,128]{1,0:T(8,128)(2,1)S(1)}, bf16[96,128,128]{2,1,0:T(8,128)(2,1)S(1)}) custom-call(s32[4,96]{1,0:T(4,128)S(1)} %copy-done.7, s32[96]{0:T(128)S(1)} %fusion.4.home_ref, bf16[128,3072]{1,0:T(8,128)(2,1)S(1)} %bitcast.40, ...), custom_call_target="tpu_custom_call" | custom-call | flops 1000000000 | bytes 10000000 | tf_op jit(solution)/shard_map/butterfly_down/pallas_call | solution.py:292
  106.8 1.8 copy-done
  108.6 1.6 copy-done.1
  110.2 0.9 copy-done.3
  111.1 4.3 %all-to-all-done.1.att_ref = bf16[16,128,128]{2,1,0:T(8,128)(2,1)} async-done(((bf16[16,128,128]{2,1,0:T(8,128)(2,1)}), bf16[16,128,128]{2,1,0:T(8,128)(2,1)}, u32[]{:S(2)}, u32[]{:S(2)}) %all-to-all-start.1) | async-done | bytes 524320 | tf_op jit(solution)/shard_map/all_to_all | solution.py:506
  115.5 9.8 %products.1 = (bf16[2048,128]{1,0:T(8,128)(2,1)}, bf16[128,3072]{1,0:T(8,128)(2,1)}) custom-call(bf16[2048,3072]{1,0:T(8,128)(2,1)} %all-gather.2.cloned.1.call-done.weight_ref, bf16[3072,128]{1,0:T(8,128)(2,1)} %copy-done.3, bf16[16,128,128]{2,1,0:T(8,128)(2,1)} %all-to-all-done.1.att_ref), custom_call_target="tpu_custom_call" | custom-call | flops 3221225472 | bytes 12582912 | tf_op jit(solution)/shard_map/products/pallas_call | solution.py:416
  125.2 9.9 %all-to-all-start.2 = ((bf16[16,128,128]{2,1,0:T(8,128)(2,1)}), bf16[16,128,128]{2,1,0:T(8,128)(2,1)S(1)}, u32[]{:S(2)}, u32[]{:S(2)}) async-start(bf16[16,128,128]{2,1,0:T(8,128)(2,1)} %bitcast.45), calls=%async_computation.2 | async-start | bytes 1048576 | tf_op jit(solution)/shard_map/all_to_all | solution.py:510
  135.8 10.6 %butterfly_up.1 = (bf16[128,3072]{1,0:T(8,128)(2,1)}, bf16[8,6,128,128]{3,2,1,0:T(8,128)(2,1)}, bf16[8,6,128,128]{3,2,1,0:T(8,128)(2,1)}) custom-call(s32[4,96]{1,0:T(4,128)} %order_ref.3, s32[3]{0:T(128)} %pad_add_fusion.self_ref, bf16[128,3072]{1,0:T(8,128)(2,1)} %get-tuple-element.34.proj_ref, bf16[96,128,128]{2,1,0:T(8,128)(2,1)} %copy-done.1, ...), custom_call_target="tpu_custom_call" | custom-call | flops 1000000000 | bytes 10000000 | tf_op jit(solution)/shard_map/butterfly_up/pallas_call | solution.py:368
  146.5 6.1 %all-to-all-done.2.dout_ref = bf16[16,128,128]{2,1,0:T(8,128)(2,1)S(1)} async-done(((bf16[16,128,128]{2,1,0:T(8,128)(2,1)}), bf16[16,128,128]{2,1,0:T(8,128)(2,1)S(1)}, u32[]{:S(2)}, u32[]{:S(2)}) %all-to-all-start.2) | async-done | bytes 524320 | tf_op jit(solution)/shard_map/all_to_all | solution.py:510
  152.6 0.8 copy-done.9
  153.4 12.4 %attend_back.1 = bf16[16,3,128,128]{3,2,1,0:T(8,128)(2,1)} custom-call(bf16[16,3,128,128]{3,2,1,0:T(8,128)(2,1)} %copy-done.8, bf16[16,3,128,128]{3,2,1,0:T(8,128)(2,1)} %copy-done.8, bf16[16,3,128,128]{3,2,1,0:T(8,128)(2,1)} %copy-done.8, bf16[16,128,128]{2,1,0:T(8,128)(2,1)} %copy-done.9, f32[4,128,512]{2,1,0:T(8,128)} %get-tuple-element.43.wide_ref, ...), custom_call_target="tpu_custom_call" | custom-call | flops 4294967296 | bytes 8388608 | tf_op jit(solution)/shard_map/attend_back/pallas_call | solution.py:213
  165.8 5.0 %all-to-all-start.3 = ((bf16[16,3,128,128]{3,2,1,0:T(8,128)(2,1)}), bf16[16,3,128,128]{3,2,1,0:T(8,128)(2,1)S(1)}, u32[]{:S(2)}, u32[]{:S(2)}) async-start(bf16[16,3,128,128]{3,2,1,0:T(8,128)(2,1)} %attend_back.1), calls=%async_computation.3 | async-start | bytes 3145728 | tf_op jit(solution)/shard_map/all_to_all | solution.py:518
  170.8 1.4 add_convert_fusion.1
  172.4 3.2 %collective-permute-start.9 = (bf16[2,6,128,128]{3,2,1,0:T(8,128)(2,1)S(1)}, bf16[2,6,128,128]{3,2,1,0:T(8,128)(2,1)S(1)}, u32[]{:S(2)}, u32[]{:S(2)}) collective-permute-start(bf16[2,6,128,128]{3,2,1,0:T(8,128)(2,1)S(1)} %get-tuple-element.58), channel_id=1, source_target_pairs={{0,136},{128,0},{8,128},{136,8},{1,137},{129,1},{9,129},{137,9},{2... | collective-permute-start | bytes 1179656 | tf_op jit(solution)/shard_map/ppermute | solution.py:453
  175.6 15.7 %collective-permute-done.8 = bf16[2,6,128,128]{3,2,1,0:T(8,128)(2,1)S(1)} collective-permute-done((bf16[2,6,128,128]{3,2,1,0:T(8,128)(2,1)S(1)}, bf16[2,6,128,128]{3,2,1,0:T(8,128)(2,1)S(1)}, u32[]{:S(2)}, u32[]{:S(2)}) %collective-permute-start.8) | collective-permute-done | bytes 393248 | tf_op jit(solution)/shard_map/ppermute | solution.py:453
  191.2 1.5 add_convert_fusion
  193.1 2.0 collective-permute-start.12
  195.0 7.2 %collective-permute-done.10 = bf16[6,128,128]{2,1,0:T(8,128)(2,1)S(1)} collective-permute-done((bf16[6,128,128]{2,1,0:T(8,128)(2,1)S(1)}, bf16[6,128,128]{2,1,0:T(8,128)(2,1)S(1)}, u32[]{:S(2)}, u32[]{:S(2)}) %collective-permute-start.10) | collective-permute-done | bytes 196640 | tf_op jit(solution)/shard_map/ppermute | solution.py:447
  202.7 2.5 collective-permute-done.12
  205.3 5.3 %all-to-all-done.3 = bf16[16,3,128,128]{3,2,1,0:T(8,128)(2,1)S(1)} async-done(((bf16[16,3,128,128]{3,2,1,0:T(8,128)(2,1)}), bf16[16,3,128,128]{3,2,1,0:T(8,128)(2,1)S(1)}, u32[]{:S(2)}, u32[]{:S(2)}) %all-to-all-start.3) | async-done | bytes 1572896 | tf_op jit(solution)/shard_map/all_to_all | solution.py:518
  210.6 15.2 %all_to_all.30 = bf16[16,48,128]{2,1,0:T(8,128)(2,1)S(1)} all-to-all(bf16[16,48,128]{2,1,0:T(8,128)(2,1)S(1)} %bitcast.44), channel_id=1, replica_groups=mesh['xl'=2,'y'=4,'c'=2,'xh'=2,'z'=8] {'xh','z'}, dimensions={0} | all-to-all | bytes 393216 | tf_op jit(solution)/shard_map/all_to_all | solution.py:524
  225.8 0.7 broadcast_in_dim.14
  226.5 4.4 %all-to-all-start.5 = ((bf16[16,48,128]{2,1,0:T(8,128)(2,1)}), bf16[16,48,128]{2,1,0:T(8,128)(2,1)S(1)}, u32[]{:S(2)}, u32[]{:S(2)}) async-start(bf16[16,48,128]{2,1,0:T(8,128)(2,1)} %broadcast_in_dim.14), calls=%async_computation.5 | async-start | bytes 393216 | tf_op jit(solution)/shard_map/all_to_all | solution.py:529
  230.9 0.9 copy.11
  231.8 1.6 copy.12
  233.4 7.9 %all-to-all-done.5 = bf16[16,48,128]{2,1,0:T(8,128)(2,1)S(1)} async-done(((bf16[16,48,128]{2,1,0:T(8,128)(2,1)}), bf16[16,48,128]{2,1,0:T(8,128)(2,1)S(1)}, u32[]{:S(2)}, u32[]{:S(2)}) %all-to-all-start.5) | async-done | bytes 196640 | tf_op jit(solution)/shard_map/all_to_all | solution.py:529
  241.3 1.9 cayley_pullback.1
  (45 shorter events, 3.0 us)
Async XLA Ops:
  7.2 108.3 %all-gather.2.cloned.1.call-start = ((), (), s32[]{:S(2)}) async-start(), calls=%async_computation.6 | async-start | bytes 13369344 | tf_op jit(solution)/shard_map/all_gather | solution.py:498
  11.4 11.2 %copy-start.4 = (f32[6,128,128]{2,1,0:T(8,128)S(1)}, f32[6,128,128]{2,1,0:T(8,128)}, u32[]{:S(2)}) copy-start(f32[6,128,128]{2,1,0:T(8,128)} %skew_ref) | copy-start | bytes 1179652
  11.4 64.1 %all-to-all-start = ((bf16[16,3,128,128]{3,2,1,0:T(8,128)(2,1)}), bf16[16,3,128,128]{3,2,1,0:T(8,128)(2,1)S(1)}, u32[]{:S(2)}, u32[]{:S(2)}) async-start(bf16[16,3,128,128]{3,2,1,0:T(8,128)(2,1)} %bitcast.6), calls=%async_computation | async-start | bytes 3145728 | tf_op jit(solution)/shard_map/all_to_all | solution.py:500
  36.6 23.2 %copy-start.5 = (f32[6,128,128]{2,1,0:T(8,128)}, f32[6,128,128]{2,1,0:T(8,128)S(1)}, u32[]{:S(2)}) copy-start(f32[6,128,128]{2,1,0:T(8,128)S(1)} %get-tuple-element.47.inv_ref) | copy-start | bytes 1179652
  36.6 11.6 %collective-permute-start = (bf16[6,128,128]{2,1,0:T(8,128)(2,1)S(1)}, bf16[6,128,128]{2,1,0:T(8,128)(2,1)S(1)}, u32[]{:S(2)}, u32[]{:S(2)}) collective-permute-start(bf16[6,128,128]{2,1,0:T(8,128)(2,1)S(1)} %get-tuple-element.28), channel_id=1, source_target_pairs={{0,32},{32,64},{64,96},{96,0},{1,33},{33,65},{65,97},{97,1},{2,34}... | collective-permute-start | bytes 589832 | tf_op jit(solution)/shard_map/ppermute | solution.py:447
  36.9 11.4 %collective-permute-start.1 = (bf16[6,128,128]{2,1,0:T(8,128)(2,1)S(1)}, bf16[6,128,128]{2,1,0:T(8,128)(2,1)S(1)}, u32[]{:S(2)}, u32[]{:S(2)}) collective-permute-start(bf16[6,128,128]{2,1,0:T(8,128)(2,1)S(1)} %get-tuple-element.28), channel_id=1, source_target_pairs={{0,96},{32,0},{64,32},{96,64},{1,97},{33,1},{65,33},{97,65},{2,98}... | collective-permute-start | bytes 589832 | tf_op jit(solution)/shard_map/ppermute | solution.py:447
  48.2 7.1 %collective-permute-start.2 = (bf16[3,128,128]{2,1,0:T(8,128)(2,1)S(1)}, bf16[3,128,128]{2,1,0:T(8,128)(2,1)S(1)}, u32[]{:S(2)}, u32[]{:S(2)}) collective-permute-start(bf16[3,128,128]{2,1,0:T(8,128)(2,1)S(1)} %slice.121), channel_id=1, source_target_pairs={{0,32},{32,64},{64,96},{96,0},{1,33},{33,65},{65,97},{97,1},{2,34}... | collective-permute-start | bytes 294920 | tf_op jit(solution)/shard_map/ppermute | solution.py:447
  48.3 7.0 %collective-permute-start.3 = (bf16[3,128,128]{2,1,0:T(8,128)(2,1)S(1)}, bf16[3,128,128]{2,1,0:T(8,128)(2,1)S(1)}, u32[]{:S(2)}, u32[]{:S(2)}) collective-permute-start(bf16[3,128,128]{2,1,0:T(8,128)(2,1)S(1)} %slice.122), channel_id=1, source_target_pairs={{0,96},{32,0},{64,32},{96,64},{1,97},{33,1},{65,33},{97,65},{2,98}... | collective-permute-start | bytes 294920 | tf_op jit(solution)/shard_map/ppermute | solution.py:447
  50.4 19.7 %collective-permute-start.4 = (bf16[12,128,128]{2,1,0:T(8,128)(2,1)S(1)}, bf16[12,128,128]{2,1,0:T(8,128)(2,1)S(1)}, u32[]{:S(2)}, u32[]{:S(2)}) collective-permute-start(bf16[12,128,128]{2,1,0:T(8,128)(2,1)S(1)} %pad_maximum_fusion.1), channel_id=1, source_target_pairs={{0,128},{128,8},{8,136},{136,0},{1,129},{129,9},{9,137},{137,1},{2... | collective-permute-start | bytes 1179656 | tf_op jit(solution)/shard_map/ppermute | solution.py:453
  55.3 20.1 %collective-permute-start.5 = (bf16[12,128,128]{2,1,0:T(8,128)(2,1)S(1)}, bf16[12,128,128]{2,1,0:T(8,128)(2,1)S(1)}, u32[]{:S(2)}, u32[]{:S(2)}) collective-permute-start(bf16[12,128,128]{2,1,0:T(8,128)(2,1)S(1)} %pad_maximum_fusion.2), channel_id=1, source_target_pairs={{0,136},{128,0},{8,128},{136,8},{1,137},{129,1},{9,129},{137,9},{2... | collective-permute-start | bytes 1179656 | tf_op jit(solution)/shard_map/ppermute | solution.py:453
  75.5 1.2 copy-start.8
  77.6 20.3 %copy-start.2 = (bf16[1,128,3072]{2,1,0:T(8,128)(2,1)S(1)}, bf16[1,128,3072]{2,1,0:T(8,128)(2,1)}, u32[]{:S(2)}) copy-start(bf16[1,128,3072]{2,1,0:T(8,128)(2,1)} %param.10) | copy-start | bytes 2359300
  77.6 20.3 %copy-start.7 = (s32[4,96]{1,0:T(4,128)S(1)}, s32[4,96]{1,0:T(4,128)}, u32[]{:S(2)}) copy-start(s32[4,96]{1,0:T(4,128)} %order_ref.3) | copy-start | bytes 4612
  77.6 20.2 %collective-permute-start.6 = (bf16[48,128,128]{2,1,0:T(8,128)(2,1)}, bf16[48,128,128]{2,1,0:T(8,128)(2,1)}, u32[]{:S(2)}, u32[]{:S(2)}) collective-permute-start(bf16[48,128,128]{2,1,0:T(8,128)(2,1)} %constant_dynamic-update-slice_fusion.near_ref), channel_id=1, source_target_pairs={{0,16},{16,0},{1,17},{17,1},{2,18},{18,2},{3,19},{19,3},{4,20},{20... | collective-permute-start | bytes 4718600 | tf_op jit(solution)/shard_map/ppermute | solution.py:442
  89.0 26.4 %all-to-all-start.1 = ((bf16[16,128,128]{2,1,0:T(8,128)(2,1)}), bf16[16,128,128]{2,1,0:T(8,128)(2,1)}, u32[]{:S(2)}, u32[]{:S(2)}) async-start(bf16[16,128,128]{2,1,0:T(8,128)(2,1)} %get-tuple-element.31), calls=%async_computation.1 | async-start | bytes 1048576 | tf_op jit(solution)/shard_map/all_to_all | solution.py:506
  106.8 1.8 copy-start
  108.6 1.6 copy-start.1
  110.2 0.9 copy-start.3
  125.2 27.3 %all-to-all-start.2 = ((bf16[16,128,128]{2,1,0:T(8,128)(2,1)}), bf16[16,128,128]{2,1,0:T(8,128)(2,1)S(1)}, u32[]{:S(2)}, u32[]{:S(2)}) async-start(bf16[16,128,128]{2,1,0:T(8,128)(2,1)} %bitcast.45), calls=%async_computation.2 | async-start | bytes 1048576 | tf_op jit(solution)/shard_map/all_to_all | solution.py:510
  152.5 0.9 copy-start.9
  152.6 13.3 %collective-permute-start.7 = (bf16[8,6,128,128]{3,2,1,0:T(8,128)(2,1)}, bf16[8,6,128,128]{3,2,1,0:T(8,128)(2,1)}, u32[]{:S(2)}, u32[]{:S(2)}) collective-permute-start(bf16[8,6,128,128]{3,2,1,0:T(8,128)(2,1)} %get-tuple-element.41), channel_id=1, source_target_pairs={{0,16},{16,0},{1,17},{17,1},{2,18},{18,2},{3,19},{19,3},{4,20},{20... | collective-permute-start | bytes 4718600 | tf_op jit(solution)/shard_map/ppermute | solution.py:442
  165.8 5.0 %copy-start.10 = (bf16[8,6,128,128]{3,2,1,0:T(8,128)(2,1)S(1)}, bf16[8,6,128,128]{3,2,1,0:T(8,128)(2,1)}, u32[]{:S(2)}) copy-start(bf16[8,6,128,128]{3,2,1,0:T(8,128)(2,1)} %get-tuple-element.48) | copy-start | bytes 4718596
  165.8 44.7 %all-to-all-start.3 = ((bf16[16,3,128,128]{3,2,1,0:T(8,128)(2,1)}), bf16[16,3,128,128]{3,2,1,0:T(8,128)(2,1)S(1)}, u32[]{:S(2)}, u32[]{:S(2)}) async-start(bf16[16,3,128,128]{3,2,1,0:T(8,128)(2,1)} %attend_back.1), calls=%async_computation.3 | async-start | bytes 3145728 | tf_op jit(solution)/shard_map/all_to_all | solution.py:518
  172.3 19.0 %collective-permute-start.8 = (bf16[2,6,128,128]{3,2,1,0:T(8,128)(2,1)S(1)}, bf16[2,6,128,128]{3,2,1,0:T(8,128)(2,1)S(1)}, u32[]{:S(2)}, u32[]{:S(2)}) collective-permute-start(bf16[2,6,128,128]{3,2,1,0:T(8,128)(2,1)S(1)} %get-tuple-element.57), channel_id=1, source_target_pairs={{0,128},{128,8},{8,136},{136,0},{1,129},{129,9},{9,137},{137,1},{2... | collective-permute-start | bytes 1179656 | tf_op jit(solution)/shard_map/ppermute | solution.py:453
  172.4 18.8 %collective-permute-start.9 = (bf16[2,6,128,128]{3,2,1,0:T(8,128)(2,1)S(1)}, bf16[2,6,128,128]{3,2,1,0:T(8,128)(2,1)S(1)}, u32[]{:S(2)}, u32[]{:S(2)}) collective-permute-start(bf16[2,6,128,128]{3,2,1,0:T(8,128)(2,1)S(1)} %get-tuple-element.58), channel_id=1, source_target_pairs={{0,136},{128,0},{8,128},{136,8},{1,137},{129,1},{9,129},{137,9},{2... | collective-permute-start | bytes 1179656 | tf_op jit(solution)/shard_map/ppermute | solution.py:453
  192.8 9.4 %collective-permute-start.10 = (bf16[6,128,128]{2,1,0:T(8,128)(2,1)S(1)}, bf16[6,128,128]{2,1,0:T(8,128)(2,1)S(1)}, u32[]{:S(2)}, u32[]{:S(2)}) collective-permute-start(bf16[6,128,128]{2,1,0:T(8,128)(2,1)S(1)} %get-tuple-element.54), channel_id=1, source_target_pairs={{0,64},{32,96},{64,0},{96,32},{1,65},{33,97},{65,1},{97,33},{2,66}... | collective-permute-start | bytes 589832 | tf_op jit(solution)/shard_map/ppermute | solution.py:447
  192.9 9.7 %collective-permute-start.11 = (bf16[6,128,128]{2,1,0:T(8,128)(2,1)S(1)}, bf16[6,128,128]{2,1,0:T(8,128)(2,1)S(1)}, u32[]{:S(2)}, u32[]{:S(2)}) collective-permute-start(bf16[6,128,128]{2,1,0:T(8,128)(2,1)S(1)} %get-tuple-element.56), channel_id=1, source_target_pairs={{0,32},{32,64},{64,96},{96,0},{1,33},{33,65},{65,97},{97,1},{2,34}... | collective-permute-start | bytes 589832 | tf_op jit(solution)/shard_map/ppermute | solution.py:447
  193.1 12.1 %collective-permute-start.12 = (bf16[6,128,128]{2,1,0:T(8,128)(2,1)S(1)}, bf16[6,128,128]{2,1,0:T(8,128)(2,1)S(1)}, u32[]{:S(2)}, u32[]{:S(2)}) collective-permute-start(bf16[6,128,128]{2,1,0:T(8,128)(2,1)S(1)} %get-tuple-element.55), channel_id=1, source_target_pairs={{0,96},{32,0},{64,32},{96,64},{1,97},{33,1},{65,33},{97,65},{2,98}... | collective-permute-start | bytes 589832 | tf_op jit(solution)/shard_map/ppermute | solution.py:447
  226.5 14.8 %all-to-all-start.5 = ((bf16[16,48,128]{2,1,0:T(8,128)(2,1)}), bf16[16,48,128]{2,1,0:T(8,128)(2,1)S(1)}, u32[]{:S(2)}, u32[]{:S(2)}) async-start(bf16[16,48,128]{2,1,0:T(8,128)(2,1)} %broadcast_in_dim.14), calls=%async_computation.5 | async-start | bytes 393216 | tf_op jit(solution)/shard_map/all_to_all | solution.py:529
  231.8 9.5 %copy-start.6 = (f32[6,128,128]{2,1,0:T(8,128)S(1)}, f32[6,128,128]{2,1,0:T(8,128)}, u32[]{:S(2)}) copy-start(f32[6,128,128]{2,1,0:T(8,128)} %copy-done.5) | copy-start | bytes 1179652
Sparse Core Ops, SparseCore 0:
  9.8 105.5 all-gather.1
